TPU v7x, 128 devices: a whole 4x4x4 slice. The times are simulated.
128 devices in a mesh: slab: 32 (over y_hi, z, x), lvl: 4 (over y_lo, core).
Axes of the slice: x: 4, y: 4 (y_hi: 2, y_lo: 2; y = y_hi * 2 + y_lo), z: 4, core: 2. Of those that a mesh axis runs over, the one named last changes fastest.
Arguments:
- fine_state: float32 [32, 4, 5, 32, 1024], P('slab', 'lvl'), as said below
- coarse_state: float32 [32, 4, 5, 32, 1024], P('slab', 'lvl'), as said below
- partner: int32 [32, 4], P(None, 'lvl'), may hold values from 0 to 31, as said below
- mig_slot: int32 [32, 4], P(None, 'lvl'), may hold values from 0 to 0
- neighbours: int32 [32, 4, 6], P(None, 'lvl'), may hold values from -1 to 31, as said below
- work: int32 [32, 4], P(None, 'lvl'), may hold values from 1 to 4
- coarse_link: int32 [32, 4], P('slab', 'lvl'), may hold values from -1 to 95, as said below
Outputs:
- fine_out: float32 [32, 4, 5, 32, 1024], P('slab', 'lvl')
- coarse_out: float32 [32, 4, 5, 32, 1024], P('slab', 'lvl')
Inputs may be any that keep to these rules, and one draw needn't show every extreme that they name: `fine_state`: density and pressure of every cell lie in 0.6 .. 1.5 and each velocity component in -0.3 .. 0.3; the arrays hold density, the three momenta and the total energy for a ratio of specific heats of 1.4. `coarse_state`: same law as the fine patches. An involution: partner[s, l] is s (no migration) or s XOR 2 ** b for some bit b; in every lvl column every bit of the slab index is used by some pair. `neighbours`: codes are slot codes before migration, -1 where there is no fine neighbour; symmetric: if the patch at code a has b across face f, then b has a across face f XOR 1. The fine patches of one lvl index form a lattice of 8 by 2 by 2 patches. `coarse_link`: -1 or c * 24 + f * 4 + q with c a lvl index, f a face of the fine patch and q a quarter of the coarse face; several fine faces may name the same place.
All inputs are finite; a program needn't handle non-finite values.
Results may differ from a plain program's by a relative error of at most 0.0003.
Values sent between devices are 32-bit elements; how exact they have to be, the bound alone decides.
A program may use at most 192 MiB of HBM per device.

v0:
```python
import jax
import jax.numpy as jnp
from jax import lax
from jax.sharding import PartitionSpec as P

ADIABATIC = 1.4
COARSE_STEP = 0.035
FLIPPED = (1, 0, 3, 2, 5, 4)
SIGNS = (-1.0, 1.0, -1.0, 1.0, -1.0, 1.0)
HIGHEST = lax.Precision.HIGHEST


def euler_flux(conserved, direction):
    density = conserved[..., 0, :, :, :]
    momenta = conserved[..., 1:4, :, :, :]
    energy = conserved[..., 4, :, :, :]
    velocity = momenta / density[..., None, :, :, :]
    kinetic = 0.5 * jnp.sum(momenta * velocity, axis=-4)
    pressure = (ADIABATIC - 1.0) * (energy - kinetic)
    normal = velocity[..., direction, :, :, :]
    wave_speed = jnp.abs(normal) + jnp.sqrt(ADIABATIC * pressure / density)
    momentum_flux = momenta * normal[..., None, :, :, :]
    momentum_flux = momentum_flux.at[..., direction, :, :, :].add(pressure)
    mass_flux = momenta[..., direction, :, :, :]
    energy_flux = (energy + pressure) * normal
    flux_all = jnp.concatenate(
        [mass_flux[..., None, :, :, :], momentum_flux, energy_flux[..., None, :, :, :]], axis=-4
    )
    return (flux_all, wave_speed)


def rusanov(left_side, right_side, direction):
    flux_left, speed_left = euler_flux(left_side, direction)
    flux_right, speed_right = euler_flux(right_side, direction)
    fastest = jnp.maximum(speed_left, speed_right)
    return 0.5 * (flux_left + flux_right) - 0.5 * fastest[..., None, :, :, :] * (
        right_side - left_side
    )


def advance(conserved, ghosts):
    divergence = None
    boundary = []
    for direction in range(3):
        spatial = conserved.ndim - 3 + direction
        lower_face = jnp.expand_dims(ghosts[..., 2 * direction, :, :, :], spatial)
        upper_face = jnp.expand_dims(ghosts[..., 2 * direction + 1, :, :, :], spatial)
        extended = jnp.concatenate([lower_face, conserved, upper_face], axis=spatial)
        cells_plus = extended.shape[spatial]
        left_side = lax.slice_in_dim(extended, 0, cells_plus - 1, axis=spatial)
        right_side = lax.slice_in_dim(extended, 1, cells_plus, axis=spatial)
        interface = rusanov(left_side, right_side, direction)
        faces_along = interface.shape[spatial]
        change = lax.slice_in_dim(interface, 1, faces_along, axis=spatial) - lax.slice_in_dim(
            interface, 0, faces_along - 1, axis=spatial
        )
        divergence = change if divergence is None else divergence + change
        boundary.append(lax.index_in_dim(interface, 0, spatial, keepdims=False))
        boundary.append(lax.index_in_dim(interface, faces_along - 1, spatial, keepdims=False))
    return (divergence, jnp.stack(boundary, axis=-4))


def face_layers(conserved):
    return jnp.stack(
        [
            conserved[..., 0, :, :],
            conserved[..., -1, :, :],
            conserved[..., :, 0, :],
            conserved[..., :, -1, :],
            conserved[..., :, :, 0],
            conserved[..., :, :, -1],
        ],
        axis=-4,
    )


def coarsen(faces):
    half_cells = faces.shape[-1] // 2
    blocks = faces.reshape(faces.shape[:-2] + (half_cells, 2, half_cells, 2))
    return 0.25 * (
        blocks[..., 0, :, 0] + blocks[..., 1, :, 0] + blocks[..., 0, :, 1] + blocks[..., 1, :, 1]
    )


def place_quarters(quartered):
    leading = quartered.shape[:-4]
    half_cells = quartered.shape[-1]
    fields = quartered.shape[-3]
    quarter_grid = quartered.reshape(leading + (2, 2, fields, half_cells, half_cells))
    grid_rank = quarter_grid.ndim
    axis_order = tuple(range(grid_rank - 5)) + (
        grid_rank - 3,
        grid_rank - 5,
        grid_rank - 2,
        grid_rank - 4,
        grid_rank - 1,
    )
    return jnp.transpose(quarter_grid, axis_order).reshape(
        leading + (fields, 2 * half_cells, 2 * half_cells)
    )


def expand_cover(counted, half_cells):
    leading = counted.shape[:-1]
    quarter_grid = counted.reshape(leading + (2, 2))
    spread_out = jnp.broadcast_to(
        quarter_grid[..., :, None, :, None], leading + (2, half_cells, 2, half_cells)
    )
    return spread_out.reshape(leading + (2 * half_cells, 2 * half_cells))


def apply_correction(advanced, coarse_flux, totals, cover_full):
    for face_index in range(6):
        amount = (
            SIGNS[face_index]
            * COARSE_STEP
            * (
                cover_full[..., face_index, None, :, :] * coarse_flux[..., face_index, :, :, :]
                - totals[..., face_index, :, :, :]
            )
        )
        edge_index = 0 if face_index % 2 == 0 else -1
        if face_index // 2 == 0:
            advanced = advanced.at[..., edge_index, :, :].add(amount)
        elif face_index // 2 == 1:
            advanced = advanced.at[..., :, edge_index, :].add(amount)
        else:
            advanced = advanced.at[..., :, :, edge_index].add(amount)
    return advanced


def body(fine_state, coarse_state, partner, mig_slot, neighbours, work, coarse_link):
    slab_index = lax.axis_index("slab")
    slab_count = lax.axis_size("slab")
    lvl_count = lax.axis_size("lvl")
    per_device = fine_state.shape[0]
    fields = fine_state.shape[2]
    edge_cells = fine_state.shape[3]
    total_slots = neighbours.shape[0]
    resident_flat = fine_state[:, 0]
    partner_col = partner[:, 0]
    mig_col = mig_slot[:, 0]
    slab_iota = jnp.arange(slab_count, dtype=jnp.int32)
    mate_slab = jnp.sum(jnp.where(slab_iota == slab_index, partner_col, 0))
    my_slot = jnp.sum(jnp.where(slab_iota == slab_index, mig_col, 0))
    outgoing = lax.dynamic_index_in_dim(resident_flat, my_slot, 0, keepdims=True)
    portion = lax.all_gather(outgoing, "slab", axis=0, tiled=True)
    inside = (mate_slab >= 0) & (mate_slab < portion.shape[0])
    picked = lax.dynamic_index_in_dim(
        portion, jnp.clip(mate_slab, 0, portion.shape[0] - 1), 0, keepdims=True
    )
    arrived = jnp.where(inside, picked, 0.0)
    migrated_flat = lax.dynamic_update_index_in_dim(resident_flat, arrived[0], my_slot, 0)
    migrated = migrated_flat.reshape(per_device, fields, edge_cells, edge_cells, edge_cells)

    def relocate_codes(slot_codes):
        clipped = jnp.maximum(slot_codes, 0)
        owner_slab = clipped // per_device
        owner_hits = owner_slab[..., None] == slab_iota
        owner_mate = jnp.sum(jnp.where(owner_hits, partner_col, 0), axis=-1)
        owner_slot = jnp.sum(jnp.where(owner_hits, mig_col, 0), axis=-1)
        mate_slot_of = jnp.sum(jnp.where(owner_mate[..., None] == slab_iota, mig_col, 0), axis=-1)
        shifted = jnp.where(
            clipped % per_device == owner_slot, owner_mate * per_device + mate_slot_of, slot_codes
        )
        return jnp.where(slot_codes < 0, slot_codes, shifted)

    slots_iota = jnp.arange(total_slots, dtype=jnp.int32)
    anchor_all = relocate_codes(slots_iota)
    slot_hits = (anchor_all[:, None] == slots_iota[None, :]).astype(jnp.int32)
    work_all = jnp.sum(slot_hits * work[:, 0][None, :], axis=1)
    before_all = jnp.sum(slot_hits[:, :, None] * neighbours[:, 0, :][None, :, :], axis=1)
    step_count = lax.dynamic_slice_in_dim(work_all, slab_index * per_device, per_device, 0)
    own_layers = face_layers(migrated)
    empty_faces = jnp.zeros(own_layers.shape, jnp.float32)
    targets_all = relocate_codes(before_all)
    outgoing_faces = own_layers.reshape(per_device, 6, fields, edge_cells * edge_cells)
    targets = lax.dynamic_slice_in_dim(targets_all, slab_index * per_device, per_device, 0)

    def collect_faces(portion):
        shaped = portion.reshape(portion.shape[:3] + (edge_cells, edge_cells))
        mirrored = jnp.stack([shaped[:, face_index] for face_index in FLIPPED], axis=1)
        row_codes = jnp.arange(portion.shape[0], dtype=jnp.int32)
        chooser = (targets[:, :, None] == row_codes[None, None, :]).astype(jnp.float32)
        return jnp.einsum("pfr,rfxab->pfxab", chooser, mirrored, precision=HIGHEST)

    fetched = collect_faces(lax.all_gather(outgoing_faces, "slab", axis=0, tiled=True))
    ghosts = jnp.where((targets >= 0)[:, :, None, None, None], fetched, own_layers)
    step_float = step_count.astype(jnp.float32)
    step_ratio = 2.0 * COARSE_STEP / step_float
    ratio_wide = step_ratio[:, None, None, None, None]
    count_wide = step_float[:, None, None, None, None]

    def one_substep(substep, carried):
        current, register = carried
        divergence, boundary = advance(current, ghosts)
        active = (substep < step_count)[:, None, None, None, None]
        register_next = jnp.where(active, register + boundary / count_wide, register)
        current_next = jnp.where(active, current - ratio_wide * divergence, current)
        return (current_next, register_next)

    final_state, register = lax.fori_loop(
        0, jnp.max(step_count), one_substep, (migrated, empty_faces)
    )
    coarse_code = coarse_link[:, 0]
    chooser = (coarse_code[:, None] == jnp.arange(lvl_count * 24, dtype=jnp.int32)[None, :]).astype(
        jnp.float32
    )
    chooser = chooser.reshape(per_device, lvl_count, 6, 4)
    coarsened = coarsen(register)
    summed = jnp.einsum("pcfq,pfxab->cfqxab", chooser, coarsened, precision=HIGHEST)
    counted = jnp.sum(chooser, axis=0)
    summed = jnp.stack([summed[:, face_index] for face_index in FLIPPED], axis=1)
    counted = jnp.stack([counted[:, face_index] for face_index in FLIPPED], axis=1)
    flux_term = place_quarters(summed).reshape(lvl_count, 6, fields, edge_cells * edge_cells)
    owned_flux, owned_cover = (
        lax.psum_scatter(flux_term, "lvl", scatter_dimension=0, tiled=True),
        lax.psum_scatter(counted, "lvl", scatter_dimension=0, tiled=True),
    )
    coarse_local = coarse_state[0, 0].reshape(fields, edge_cells, edge_cells, edge_cells)
    coarse_ghosts = face_layers(coarse_local)
    divergence, coarse_flux = advance(coarse_local, coarse_ghosts)
    advanced = coarse_local - COARSE_STEP * divergence
    totals = owned_flux[0].reshape(6, fields, edge_cells, edge_cells)
    cover_full = expand_cover(owned_cover[0], edge_cells // 2)
    coarse_out = apply_correction(advanced, coarse_flux, totals, cover_full)
    fine_out = final_state.reshape(per_device, 1, fields, edge_cells, edge_cells * edge_cells)
    return (fine_out, coarse_out.reshape(1, 1, fields, edge_cells, edge_cells * edge_cells))


def solution(mesh):
    return jax.shard_map(
        body,
        mesh=mesh,
        in_specs=(
            P("slab", "lvl", None, None, None),
            P("slab", "lvl", None, None, None),
            P(None, "lvl"),
            P(None, "lvl"),
            P(None, "lvl", None),
            P(None, "lvl"),
            P("slab", "lvl"),
        ),
        out_specs=(P("slab", "lvl", None, None, None), P("slab", "lvl", None, None, None)),
        check_vma=False,
    )
```

profile of v0, /device:TPU:1, one launch (start us, length us, event | category | flops | bytes accessed | tf_op | source)
XLA Modules:
  0.0 680.3 jit_solution(13501125196182957413)
XLA Ops:
  19.4 3.1 reshape_squeeze.4
  22.6 3.3 copy.303
  26.7 7.2 %all-reduce = f32[4,6,4]{1,2,0:T(4,128)S(1)} all-reduce(f32[4,6,4]{1,2,0:T(4,128)S(1)} %stack.68), channel_id=3, replica_groups=mesh['slab'=32,'lvl'=4] {'lvl'}, use_global_device_ids=true, to_apply=%region_23.24.clone | all-reduce | flops 96 | bytes 768
  42.0 2.1 fusion.97
  47.8 2.7 multiply_reduce_fusion.10
  52.1 2.6 broadcast_multiply_fusion.10
  54.8 2.1 fusion.104
  56.9 138.3 %all-gather.6.cloned.1.call-done = f32[32,1,5,32,1024]{4,3,2,1,0:T(8,128)} async-done(((f32[1,1,5,32,1024]{4,3,2,1,0:T(8,128)}), f32[32,1,5,32,1024]{4,3,2,1,0:T(8,128)}) %all-gather.6.cloned.1.call-update) | async-done | bytes 20971536 | tf_op jit(solution)/shard_map/all_gather | solution.py:147
  195.2 2.0 dynamic-slice_select_fusion
  197.1 3.1 reshape.2065
  200.2 2.7 fusion.133
  202.9 5.3 slice_reduce_fusion
  218.5 1.6 stack.59
  220.7 2.0 multiply_reduce_fusion.8
  229.3 2.4 multiply_bitcast_fusion.6
  231.7 4.1 fusion.73
  237.1 2.6 fusion.60
  240.9 2.8 fusion.56
  243.7 2.7 copy.289
  248.3 55.9 %all-gather.4.cloned.1.call-done = f32[32,6,5,1024]{3,1,2,0:T(8,128)} async-done(((f32[1,6,5,1024]{3,1,2,0:T(8,128)}), f32[32,6,5,1024]{3,1,2,0:T(8,128)}) %all-gather.4.cloned.1.call-update) | async-done | bytes 3932176 | tf_op jit(solution)/shard_map/all_gather | solution.py:187
  304.3 6.7 copy.288
  310.9 11.2 %reshape.2066 = f32[32,6,5,32,32]{4,3,0,2,1:T(8,128)} reshape(f32[32,6,5,1024]{3,0,2,1:T(8,128)} %copy.288) | data formatting | bytes 7864320 | tf_op jit(solution)/shard_map/reshape | solution.py:181
  322.1 2.0 slice_dynamic-update-slice_fusion.5
  324.1 2.0 slice_dynamic-update-slice_fusion.4
  326.1 2.0 slice_dynamic-update-slice_fusion.3
  328.1 2.0 slice_dynamic-update-slice_fusion.2
  330.1 2.0 slice_dynamic-update-slice_fusion.1
  332.1 2.0 slice_dynamic-update-slice_fusion
  334.1 14.7 %fusion.52 = f32[6,1,5,32,32]{4,1,3,2,0:T(1,128)S(1)} fusion(f32[32,6,5,32,32]{4,3,0,2,1:T(8,128)S(1)} %slice_dynamic-update-slice_fusion, pred[6,32,1,1,1]{1,0,2,3,4:T(8,128)(4,1)S(1)} %copy-done.35), kind=kOutput, calls=%fused_computation.170 | convolution fusion | flops 11796480 | bytes 4055232 | tf_op jit(solution)/shard_map/pfr,rfxab->pfxab/dot_general | solution.py:185
  349.8 55.6 %while.33 = (s32[]{:T(128)}, f32[1,5,32,32,32]{3,2,1,4,0:T(8,128)S(1)}, f32[1,6,5,32,32]{4,3,2,1,0:T(8,128)S(1)}, s32[]{:T(128)}, s32[1]{0:T(128)}, /*index=5*/f...) while((s32[]{:T(128)}, ...), condition=%wide.region_16.17_spmd, body=%wide.region_9.16_spmd.sunk | while | flops 15798275 | bytes 88752480 | solution.py:202
  357.8 1.8 slice_bitcast_fusion.26
  363.5 1.6 fusion.156
  365.1 1.7 copy-done.4
  368.4 4.4 copy.347
  372.8 3.5 copy.346
  376.2 2.3 fusion.151
  379.4 1.9 multiply_reduce_fusion.17
  384.0 2.0 fusion.153
  386.0 3.3 fusion.158
  389.3 3.0 copy.352
  392.9 3.0 copy.353
  402.3 2.0 subtract_select_fusion.2
  405.4 2.5 copy.304
  407.9 5.5 fusion.129
  413.3 1.7 copy.327
  415.0 2.3 copy.328
  417.3 2.3 copy.329
  422.9 4.0 copy.310
  426.9 7.5 %reshape_reshape.3 = f32[4,6,5,1024]{3,0,2,1:T(4,128)} reshape(f32[4,6,5,2,16,2,16]{6,5,4,3,0,2,1:T(2,128)} %copy.310) | data formatting | bytes 983040 | tf_op jit(solution)/shard_map/reshape;reshape | solution.py:215
  434.4 9.2 %fusion.70 = f32[5,32,32,32]{3,1,2,0:T(8,128)} fusion(f32[5,32,32,33]{3,1,2,0:T(8,128)} %fusion.73, f32[5,32,33,32]{3,1,2,0:T(8,128)} %fusion.60, f32[5,33,32,32]{3,1,2,0:T(8,128)} %fusion.56, f32[5,32,32,32]{3,2,1,0:T(8,128)} %reshape_squeeze.4), kind=kLoop, calls=%fused_computation.222 | loop fusion | flops 1146880 | bytes 5242880 | tf_op jit(solution)/shard_map/sub | solution.py:223
  443.5 2.3 copy.290
  445.8 3.4 reshape.2067
  449.2 161.7 %all-reduce.4.cloned.1.call-done = f32[4,6,5,1024]{3,0,2,1:T(4,128)} async-done(((f32[4,6,5,1024]{3,0,2,1:T(4,128)}), f32[4,6,5,1024]{3,0,2,1:T(4,128)}) %all-reduce.4.cloned.1.call-update) | async-done | bytes 491536
  610.9 2.1 dynamic-slice_reduce_fusion
  614.6 3.7 scatter-add.76
  619.8 3.9 scatter-add.77
  624.0 3.5 copy.314
  630.7 5.1 fusion.67
  635.9 7.7 %scatter-add.82 = f32[5,32,32,32]{3,1,2,0:T(8,128)} dynamic-update-slice(f32[5,32,32,32]{3,1,2,0:T(8,128)} %fusion.108, f32[5,32,32,1]{3,1,2,0:T(8,128)} %fusion.67, s32[]{:T(128)} %constant.689.clone.1, s32[]{:T(128)} %constant.689.clone.1, s32[]{:T(128)} %constant.689.clone.1, s32[]{:T(128)} %constant.689.clone.1) | dynamic-update-slice | bytes 40964 | tf_op jit(solution)/shard_map/scatter-add | solution.py:128
  643.7 3.5 copy.316
  647.2 5.6 fusion.64
  652.8 15.6 %scatter-add.85 = f32[5,32,32,32]{3,1,2,0:T(8,128)} dynamic-update-slice(f32[5,32,32,32]{3,1,2,0:T(8,128)} %scatter-add.82, f32[5,32,32,1]{3,1,2,0:T(8,128)} %fusion.64, s32[]{:T(128)} %constant.689.clone.1, s32[]{:T(128)} %constant.689.clone.1, s32[]{:T(128)} %constant.689.clone.1, s32[]{:T(128)} %constant.693.clone.1) | dynamic-update-slice | bytes 40964 | tf_op jit(solution)/shard_map/scatter-add | solution.py:128
  668.4 3.2 copy.317
  671.6 2.0 reshape.2070
  (202 shorter events, 70.5 us)
Async XLA Ops:
  7.2 188.0 %all-gather.6.cloned.1.call-start = ((), (), s32[]{:S(2)}) async-start(), calls=%async_computation.1 | async-start | bytes 21626880 | tf_op jit(solution)/shard_map/all_gather | solution.py:147
  7.9 296.4 %all-gather.4.cloned.1.call-start = ((), (), s32[]{:S(2)}) async-start(), calls=%async_computation | async-start | bytes 5406720 | tf_op jit(solution)/shard_map/all_gather | solution.py:187
  22.6 3.3 copy-start.37
  42.0 10.2 %copy-start.8 = (f32[5,32,32,1]{3,1,2,0:T(8,128)}, f32[5,32,32,1]{3,1,2,0:T(8,128)S(1)}, u32[]{:S(2)}) copy-start(f32[5,32,32,1]{3,1,2,0:T(8,128)S(1)} %get-tuple-element.601) | copy-start | bytes 61444
  42.0 12.8 %copy-start.6 = (f32[5,32,32,1]{3,1,2,0:T(8,128)}, f32[5,32,32,1]{3,1,2,0:T(8,128)S(1)}, u32[]{:S(2)}) copy-start(f32[5,32,32,1]{3,1,2,0:T(8,128)S(1)} %get-tuple-element.602) | copy-start | bytes 61444
  50.5 1.1 copy-start.14
  50.5 1.6 copy-start.15
  220.2 390.8 %all-reduce.4.cloned.1.call-start = ((), (), s32[]{:S(2)}) async-start(), calls=%async_computation.2 | async-start | bytes 983040
  223.3 1.1 copy-start.18
  223.3 1.3 copy-start.19
  226.0 1.7 copy-start.9
  226.0 1.8 copy-start.24
  226.4 2.4 copy-start.7
  226.5 2.8 copy-start.12
  229.3 2.5 copy-start.22
  229.3 2.5 copy-start.23
  235.9 1.0 copy-start.20
  235.9 1.2 copy-start.21
  239.6 1.1 copy-start.16
  239.6 1.3 copy-start.17
  243.7 4.5 copy-start.27
  243.7 4.5 copy-start.26
  243.7 4.6 copy-start.25
  332.1 2.0 copy-start.35
  334.1 14.8 %copy-start.36 = (pred[6]{0:T(512)(128)(4,1)S(1)}, pred[6]{0:T(512)(128)(4,1)}, u32[]{:S(2)}) copy-start(pred[6]{0:T(512)(128)(4,1)} %compare_reduce_fusion) | copy-start | bytes 22
  365.1 1.7 copy-start.4
  367.6 5.1 copy-start.13
  376.2 2.4 copy-start
  376.2 3.2 copy-start.1
  386.0 3.3 copy-start.2
  399.4 1.7 copy-start.11
  399.4 2.6 copy-start.3
  399.4 2.9 copy-start.5
  413.3 8.9 %copy-start.30 = (f32[6,4,4]{2,0,1:T(8,128)S(1)}, f32[6,4,4]{2,0,1:T(8,128)}, u32[]{:S(2)}) copy-start(f32[6,4,4]{2,0,1:T(8,128)} %copy.309) | copy-start | bytes 1156
  445.8 167.3 %copy-start.34 = (f32[32,32]{1,0:T(8,128)S(1)}, f32[32,32]{1,0:T(8,128)}, u32[]{:S(2)}) copy-start(f32[32,32]{1,0:T(8,128)} %broadcast_in_dim.159) | copy-start | bytes 12292
  445.8 172.6 %copy-start.33 = (f32[32,32]{1,0:T(8,128)S(1)}, f32[32,32]{1,0:T(8,128)}, u32[]{:S(2)}) copy-start(f32[32,32]{1,0:T(8,128)} %broadcast_in_dim.161) | copy-start | bytes 12292
  449.2 178.3 %copy-start.31 = (f32[32,32]{1,0:T(8,128)S(1)}, f32[32,32]{1,0:T(8,128)}, u32[]{:S(2)}) copy-start(f32[32,32]{1,0:T(8,128)} %broadcast_in_dim.163) | copy-start | bytes 12292
  449.2 179.9 %copy-start.32 = (f32[32,32]{1,0:T(8,128)S(1)}, f32[32,32]{1,0:T(8,128)}, u32[]{:S(2)}) copy-start(f32[32,32]{1,0:T(8,128)} %broadcast_in_dim.165) | copy-start | bytes 12292
  449.2 181.5 %copy-start.10 = (f32[5,32,32,33]{3,1,2,0:T(8,128)S(1)}, f32[5,32,32,33]{3,1,2,0:T(8,128)}, u32[]{:S(2)}) copy-start(f32[5,32,32,33]{3,1,2,0:T(8,128)} %fusion.73) | copy-start | bytes 2027524
  449.2 181.5 %copy-start.29 = (f32[32,32]{0,1:T(8,128)S(1)}, f32[32,32]{0,1:T(8,128)}, u32[]{:S(2)}) copy-start(f32[32,32]{0,1:T(8,128)} %broadcast_in_dim.167) | copy-start | bytes 12292
  643.6 3.6 copy-start.28
Sparse Core Ops, SparseCore 0:
  11.1 184.0 all-gather.5
  220.3 83.9 all-gather.3
  434.5 176.3 all-reduce.3
where the time goes:
time: 686 us; the launch traced here: 680 us
  waiting for transfers between devices  357 us (52%)
  local copies, waits for them, and re-layouts  184 us (27%)
  other arithmetic  89.4 us (13%)
  between operations  17.7 us (3%)
  matrix products  14.7 us (2%)
  loops' own time  10.1 us (1%)
  blocking collectives  7.24 us (1%)
    unnamed x4, waiting for transfers between devices  162 us
    all_gather x1, waiting for transfers between devices, body(): portion = lax.all_gather(outgoing, 'slab', axis=0, tiled=True)  138 us
    all_gather x1, waiting for transfers between devices, body(): lax.all_gather(outgoing_faces, 'slab', axis=0, tiled=True)  55.9 us
    unnamed x83, local copies, waits for them, and re-layouts  29 us
    scatter-add x3, local copies, waits for them, and re-layouts, apply_correction(): advanced = advanced.at[..., :, :, edge_index].add(amount)  26.5 us
    sub x6, other arithmetic, rusanov(): 0.5 * (flux_left + flux_right)  14.8 us
    dot_general x1, matrix products, collect_faces(): return jnp.einsum('pfr,rfxab->pfxab', chooser, mirrored, precision=HIGHEST)  14.7 us
  transfers between devices with their start and end apart: 3, of which 3 were waited for; matrix products, arithmetic and copies ran while one was open for 11% of the time, Pallas kernels for 0%

commit v1 on v0

v1 whole, which is shorter than its diff:
```python
import functools

import jax
import jax.numpy as jnp
from jax import lax
from jax.experimental import pallas as pl
from jax.experimental.pallas import tpu as pltpu
from jax.sharding import PartitionSpec as P

MESH = pl.DeviceIdType.MESH
F32 = jnp.float32
COARSE_STEP = 0.035
TILE = (8, 128)
PATCH = (5, 32, 8, 128)
CHUNK = 4
PIECES = 32 // CHUNK
HALF = PIECES // 2


def lanes():
    return lax.broadcasted_iota(jnp.int32, TILE, 1)


def rows():
    return lax.broadcasted_iota(jnp.int32, TILE, 0)


def primitives(cells):
    density, mom_x, mom_y, mom_z, energy = cells
    inverse = 1.0 / density
    vel = [mom_x * inverse, mom_y * inverse, mom_z * inverse]
    kinetic = 0.5 * (mom_x * vel[0] + mom_y * vel[1] + mom_z * vel[2])
    pressure = 0.4 * (energy - kinetic)
    half_sound = 0.5 * jnp.sqrt(1.4 * pressure * inverse)
    return (*vel, pressure, half_sound)


def half_flux(cells, prims, direction):
    half_normal = 0.5 * prims[direction]
    pressure, half_sound = prims[3], prims[4]
    flux = [cells[1 + i] * half_normal for i in range(3)]
    flux[direction] = flux[direction] + 0.5 * pressure
    flux.append((cells[4] + pressure) * half_normal)
    return flux, jnp.abs(half_normal) + half_sound


def interface(low, low_flux, low_speed, high, high_flux, high_speed, direction, sign=None):
    fastest = jnp.maximum(low_speed, high_speed)
    if sign is not None:
        fastest = fastest * sign
    out = [0.5 * (low[1 + direction] + high[1 + direction]) - fastest * (high[0] - low[0])]
    for i in range(4):
        out.append((low_flux[i] + high_flux[i]) - fastest * (high[1 + i] - low[1 + i]))
    return out


def z_up(v):
    return pltpu.roll(v, 127, 1)


def z_down(v):
    return pltpu.roll(v, 1, 1)


def y_up(v):
    return pltpu.roll(jnp.where(lanes() < 32, pltpu.roll(v, 7, 0), v), 96, 1)


def y_down(v):
    return pltpu.roll(jnp.where(lanes() >= 96, pltpu.roll(v, 1, 0), v), 32, 1)


def edge_masks(direction):
    if direction == 1:
        return (rows() == 0) & (lanes() < 32), (rows() == 7) & (lanes() >= 96)
    return lanes() % 32 == 0, lanes() % 32 == 31


def face_sign(direction):
    lower = rows() < 4 if direction == 1 else lanes() % 32 < 16
    return jnp.where(lower, -1.0, 1.0).astype(F32)


def across(cells, prims, direction, outer):
    up, down = (y_up, y_down) if direction == 1 else (z_up, z_down)
    flux, speed = half_flux(cells, prims, direction)
    inner = interface(
        cells, flux, speed, [up(v) for v in cells], [up(v) for v in flux], up(speed), direction
    )
    border = outer(flux, speed)
    lower, upper = edge_masks(direction)
    change = [
        jnp.where(upper, border[i], inner[i]) - jnp.where(lower, border[i], down(inner[i])) for i in range(5)
    ]
    return change, border


def load_plane(ref, x):
    return [ref[f, x] for f in range(5)]


def sweep(state, update):
    def prepare(x):
        cells = load_plane(state, x)
        prims = primitives(cells)
        flux, speed = half_flux(cells, prims, 0)
        return cells, prims, flux, speed

    ghost, _, ghost_flux, ghost_speed = prepare(0)
    first = prepare(1)
    lowest = interface(ghost, ghost_flux, ghost_speed, first[0], first[2], first[3], 0)

    def step(x, carried):
        cells, prims, flux, speed, below = carried
        after = prepare(x + 1)
        above = interface(cells, flux, speed, after[0], after[2], after[3], 0)
        new = update(x - 1, cells, prims, [above[i] - below[i] for i in range(5)])
        for f in range(5):
            state[f, x] = new[f]
        return (*after, above)

    last = lax.fori_loop(1, 33, step, (*first, lowest))
    return lowest, last[4]


def pack_y(flat, base, side, field, stride):
    out = None
    for g in range(4):
        part = flat[pl.ds(base + field * 8 * stride + g * 8 + 7 * side, 8, stride=32), :]
        part = pltpu.roll(part, (32 * g - 96 * side) % 128, 1)
        out = part if g == 0 else jnp.where(lanes() // 32 == g, part, out)
    return out


def pack_z(plane, x, side, out):
    return jnp.where(lanes() % 32 == x, pltpu.roll(plane, (x + 128 - 31 * side) % 128, 1), out)


def spread_y(face, field, x, side):
    row = jnp.broadcast_to(face[field, pl.ds(x // 4, 1), :], TILE)
    shift = (3 - x % 4) * 32 if side else (4 - x % 4) * 32
    return pltpu.roll(row, shift % 128, 1)


def spread_z(face, field, x, side):
    return pltpu.roll(face[field], (128 - x + 31 * side) % 128, 1)


def exchange_kernel(
    partner, neighbours, fine, migrated, ghosts,
    held, relay, faces, messages, landed,
    load_sem, ghost_send, ghost_recv, near_send, near_recv, far_send, far_recv,
    up_send, up_recv, on_send, on_recv,
):
    slab = lax.axis_index("slab")
    lvl = lax.axis_index("lvl")
    loads = [
        pltpu.make_async_copy(
            fine.at[0, 0, :, :, pl.ds(j * 128, 128)], held.at[0, :, :, j, :], load_sem.at[j]
        )
        for j in range(8)
    ]
    for copy in loads:
        copy.start()

    other_lvl = lax.rem(lvl + 2, 4)
    side_a = (slab, other_lvl)
    side_b = (slab ^ 16, other_lvl)
    barrier = pltpu.get_barrier_semaphore()
    for turn in range(1, 32):
        pl.semaphore_signal(barrier, inc=1, device_id=(slab ^ turn, lvl), device_id_type=MESH)
    for device in (side_a, side_b):
        pl.semaphore_signal(barrier, inc=1, device_id=device, device_id_type=MESH)
    pl.semaphore_wait(barrier, 33)
    for copy in loads:
        copy.wait()

    own = held.at[0]
    flat = own.reshape(5 * 32 * 8, 128)
    for f in range(5):
        faces[0, f] = own[f, 0]
        faces[1, f] = own[f, 31]
        for side in range(2):
            faces[2 + side, f] = pack_y(flat, 0, side, f, 32)

    def pack(x, carried):
        return tuple(
            pack_z(own[f, x], x, side, carried[side * 5 + f]) for side in range(2) for f in range(5)
        )

    packed = lax.fori_loop(0, 32, pack, (jnp.zeros(TILE, F32),) * 10)
    for side in range(2):
        for f in range(5):
            faces[4 + side, f] = packed[side * 5 + f]

    linked = [neighbours[slab, 0, f] for f in range(6)]
    sends = []
    for turn in range(32):
        there = slab ^ turn
        patch = partner[there, 0]
        face = jnp.int32(0)
        for f in range(1, 6):
            face = jnp.where(linked[f] == patch, f, face)
        target = messages if turn else landed
        for f in range(5):
            target[turn, f] = faces[face, f]
        if turn:
            copy = pltpu.make_async_remote_copy(
                src_ref=messages.at[turn], dst_ref=landed.at[turn],
                send_sem=ghost_send.at[turn], recv_sem=ghost_recv.at[turn],
                device_id=(there, lvl), device_id_type=MESH,
            )
            copy.start()
            sends.append(copy)

    def part(ref, c):
        return ref.at[:, pl.ds(c * CHUNK, CHUNK)]

    near, far, up, on = [], [], [], []
    for c in range(PIECES):
        for axis in range(2):
            copy = pltpu.make_async_remote_copy(
                src_ref=part(own, c), dst_ref=part(held.at[1 + 2 * axis], c),
                send_sem=near_send.at[axis, c], recv_sem=near_recv.at[axis, c],
                device_id=(slab ^ (1 if axis == 0 else 4), lvl), device_id_type=MESH,
            )
            copy.start()
            near.append(copy)
        side, piece = c % 2, c // 2
        copy = pltpu.make_async_remote_copy(
            src_ref=part(own, side * HALF + piece), dst_ref=part(relay.at[side], piece),
            send_sem=up_send.at[side, piece], recv_sem=up_recv.at[side, piece],
            device_id=side_b if side else side_a, device_id_type=MESH,
        )
        copy.start()
        up.append(copy)
    for c in range(PIECES):
        for axis in range(2):
            near[c * 2 + axis].wait_recv()
            copy = pltpu.make_async_remote_copy(
                src_ref=part(held.at[1 + 2 * axis], c), dst_ref=part(held.at[2 + 2 * axis], c),
                send_sem=far_send.at[axis, c], recv_sem=far_recv.at[axis, c],
                device_id=(slab ^ (3 if axis == 0 else 12), lvl), device_id_type=MESH,
            )
            copy.start()
            far.append(copy)
        side, piece = c % 2, c // 2
        up[c].wait_recv()
        copy = pltpu.make_async_remote_copy(
            src_ref=part(relay.at[side], piece), dst_ref=part(held.at[5], side * HALF + piece),
            send_sem=on_send.at[side, piece], recv_sem=on_recv.at[side, piece],
            device_id=side_a if side else side_b, device_id_type=MESH,
        )
        copy.start()
        on.append(copy)

    for copy in sends:
        copy.wait()
    source = partner[slab, 0]
    for f in range(6):
        there = jnp.maximum(neighbours[source, 0, f], 0) ^ slab
        for i in range(5):
            ghosts[f, i] = landed[there, i]

    for copy in far:
        copy.wait()
    for copy in on:
        copy.wait()
    for copy in near:
        copy.wait_send()
    for copy in up:
        copy.wait_send()
    apart = source ^ slab
    chosen = jnp.int32(0)
    for bit in range(5):
        chosen = chosen + (apart >= (1 << bit)).astype(jnp.int32)

    def choose(x, _):
        for f in range(5):
            migrated[f, x] = held[chosen, f, x]
        return 0

    lax.fori_loop(0, 32, choose, 0)


def fine_kernel(
    partner, neighbours, work, link, migrated, ghosts, out, message,
    state, outer_y, outer_z, register, x_register, squeezed, sem, out_sem,
):
    slab = lax.axis_index("slab")
    load = pltpu.make_async_copy(migrated, state.at[:, pl.ds(1, 32)], sem)
    load.start()
    source = partner[slab, 0]
    count = work[source, 0]
    linked = [neighbours[source, 0, f] >= 0 for f in range(6)]
    step_float = count.astype(F32)
    ratio = 2.0 * COARSE_STEP / jnp.full(TILE, step_float, F32)
    share = 1.0 / jnp.full(TILE, step_float, F32)
    code = link[0, 0]
    valid = code >= 0
    level = jnp.maximum(code, 0) // 24
    face = jnp.maximum(code, 0) % 24 // 4
    quarter = jnp.maximum(code, 0) % 4
    direction, side = face // 2, face % 2
    load.wait()

    for f in range(5):
        state[f, 0] = jnp.where(linked[0], ghosts[0, f], state[f, 1])
        state[f, 33] = jnp.where(linked[1], ghosts[1, f], state[f, 32])

    def spread(x, _):
        cells = load_plane(state, x + 1)
        for d, spreader, outer in ((1, spread_y, outer_y), (2, spread_z, outer_z)):
            lower = rows() < 4 if d == 1 else lanes() % 32 < 16
            values = []
            for f in range(5):
                low = jnp.where(linked[2 * d], spreader(ghosts.at[2 * d], f, x, 0), cells[f])
                high = jnp.where(linked[2 * d + 1], spreader(ghosts.at[2 * d + 1], f, x, 1), cells[f])
                values.append(jnp.where(lower, low, high))
            flux, speed = half_flux(values, primitives(values), d)
            for i, v in enumerate(values + flux + [speed]):
                outer[i, x] = v
        return 0

    lax.fori_loop(0, 32, spread, 0)

    for substep in range(4):
        active = substep < count

        def update(x, cells, prims, change, substep=substep, active=active):
            borders = []
            for d, outer in ((1, outer_y), (2, outer_z)):

                def border(flux, speed, d=d, outer=outer):
                    return interface(
                        cells, flux, speed, [outer[i, x] for i in range(5)],
                        [outer[5 + i, x] for i in range(4)], outer[9, x], d, face_sign(d),
                    )

                part, values = across(cells, prims, d, border)
                borders.append(values)
                change = [change[i] + part[i] for i in range(5)]
            for i in range(5):
                value = jnp.where(direction == 1, borders[0][i], borders[1][i])
                value = jnp.where(active, value * share, 0.0)
                register[i, x] = value if substep == 0 else register[i, x] + value
            return [jnp.where(active, cells[i] - ratio * change[i], cells[i]) for i in range(5)]

        lowest, highest = sweep(state, update)
        for i in range(5):
            value = jnp.where(side == 0, lowest[i], highest[i])
            value = jnp.where(active, value * share, 0.0)
            x_register[i] = value if substep == 0 else x_register[i] + value

    stores = [
        pltpu.make_async_copy(
            state.at[:, pl.ds(1, 32), j, :], out.at[0, 0, :, :, pl.ds(j * 128, 128)], out_sem.at[j]
        )
        for j in range(8)
    ]
    for copy in stores:
        copy.start()

    def pack(x, carried):
        return tuple(pack_z(register[f, x], x, side, carried[f]) for f in range(5))

    packed = lax.fori_loop(0, 32, pack, (jnp.zeros(TILE, F32),) * 5)
    flat = register.reshape(5 * 32 * 8, 128)
    source_lane = lax.broadcasted_iota(jnp.int32, (128, 128), 0)
    target_lane = lax.broadcasted_iota(jnp.int32, (128, 128), 1)
    wanted = target_lane // 32 * 64 + target_lane % 32 * 2
    squeeze = ((source_lane == wanted) & (target_lane % 32 < 16) & (target_lane < 64)).astype(F32)
    for f in range(5):
        value = jnp.where(direction == 1, pack_y(flat, 0, side, f, 32), packed[f])
        value = jnp.where(direction == 0, x_register[f], value)
        value = value + pltpu.roll(value, 127, 1)
        value = 0.25 * (value + pltpu.roll(value, 96, 1))
        squeezed[pl.ds(f * 8, 8), :] = jnp.dot(
            value, squeeze, precision=lax.Precision.HIGHEST, preferred_element_type=F32
        )
    quarter_row = jnp.where(direction == 2, quarter % 2, quarter // 2)
    quarter_col = jnp.where(direction == 2, quarter // 2, quarter % 2)
    low_lanes = lax.broadcasted_iota(jnp.int32, (4, 128), 1) < 64
    for f in range(5):
        even = squeezed[pl.ds(f * 8, 4, stride=2), :]
        odd = squeezed[pl.ds(f * 8 + 1, 4, stride=2), :]
        small = jnp.where(low_lanes, even, pltpu.roll(odd, 64, 1))
        small = jnp.where(quarter_col == 0, small, pltpu.roll(small, 16, 1))
        message[f, pl.ds(0, 4), :] = jnp.where(quarter_row == 0, small, 0.0)
        message[f, pl.ds(4, 4), :] = jnp.where(quarter_row == 1, small, 0.0)
    place = level * 6 + (face ^ 1) + 1
    inside = (rows() // 4 == quarter_row) & (lanes() % 32 // 16 == quarter_col)
    message[5] = jnp.where(inside & valid, place.astype(F32), 0.0)
    for copy in stores:
        copy.wait()


def coarse_kernel(
    message, coarse, out, state, flux_y, flux_z, flux_x, landed, totals, send_sem, recv_sem, sem,
):
    slab = lax.axis_index("slab")
    lvl = lax.axis_index("lvl")
    loads = [
        pltpu.make_async_copy(
            coarse.at[0, 0, :, :, pl.ds(j * 128, 128)], state.at[:, pl.ds(1, 32), j, :], sem.at[j]
        )
        for j in range(8)
    ]
    for copy in loads:
        copy.start()
    barrier = pltpu.get_barrier_semaphore()
    for turn in range(1, 4):
        pl.semaphore_signal(barrier, inc=1, device_id=(slab, lvl ^ turn), device_id_type=MESH)
    pl.semaphore_wait(barrier, 3)
    sends = []
    for turn in range(1, 4):
        copy = pltpu.make_async_remote_copy(
            src_ref=message, dst_ref=landed.at[turn - 1],
            send_sem=send_sem.at[turn - 1], recv_sem=recv_sem.at[turn - 1],
            device_id=(slab, lvl ^ turn), device_id_type=MESH,
        )
        copy.start()
        sends.append(copy)
    for copy in loads:
        copy.wait()
    for f in range(5):
        state[f, 0] = state[f, 1]
        state[f, 33] = state[f, 32]

    def update(x, cells, prims, change):
        for d, kept in ((1, flux_y), (2, flux_z)):

            def border(flux, speed, d=d):
                return [cells[1 + d]] + [2.0 * v for v in flux]

            part, values = across(cells, prims, d, border)
            change = [change[i] + part[i] for i in range(5)]
            for i in range(5):
                kept[i, x] = values[i]
        return [cells[i] - COARSE_STEP * change[i] for i in range(5)]

    lowest, highest = sweep(state, update)
    for i in range(5):
        flux_x[0, i] = lowest[i]
        flux_x[1, i] = highest[i]
    for copy in sends:
        copy.wait()

    for g in range(6):
        key = (lvl * 6 + g + 1).astype(F32)
        hits = [(message if n == 3 else landed.at[n])[5] == key for n in range(4)]
        for f in range(5):
            total = jnp.zeros(TILE, F32)
            for n in range(4):
                total = total + jnp.where(hits[n], (message if n == 3 else landed.at[n])[f], 0.0)
            totals[g, f] = total
        cover = jnp.zeros(TILE, F32)
        for n in range(4):
            cover = cover + jnp.where(hits[n], 1.0, 0.0)
        totals[g, 5] = cover

    for side, x in ((0, 1), (1, 32)):
        for f in range(5):
            amount = totals[side, 5] * flux_x[side, f] - totals[side, f]
            state[f, x] = state[f, x] + (COARSE_STEP if side else -COARSE_STEP) * amount

    def correct(x, _):
        cells = load_plane(state, x + 1)
        for d, spreader, kept in ((1, spread_y, flux_y), (2, spread_z, flux_z)):
            lower, upper = edge_masks(d)
            weight = COARSE_STEP * face_sign(d) * (lower | upper).astype(F32)

            def both(f, d=d, spreader=spreader, upper=upper):
                low = spreader(totals.at[2 * d], f, x, 0)
                high = spreader(totals.at[2 * d + 1], f, x, 1)
                return jnp.where(upper, high, low)

            cover = both(5)
            for f in range(5):
                cells[f] = cells[f] + weight * (cover * kept[f, x] - both(f))
        for f in range(5):
            state[f, x + 1] = cells[f]
        return 0

    lax.fori_loop(0, 32, correct, 0)
    stores = [
        pltpu.make_async_copy(
            state.at[:, pl.ds(1, 32), j, :], out.at[0, 0, :, :, pl.ds(j * 128, 128)], sem.at[j]
        )
        for j in range(8)
    ]
    for copy in stores:
        copy.start()
    for copy in stores:
        copy.wait()


SMEM = pl.BlockSpec(memory_space=pltpu.SMEM)
VMEM = pl.BlockSpec(memory_space=pltpu.VMEM)
ANY = pl.BlockSpec(memory_space=pl.ANY)
DMA = pltpu.SemaphoreType.DMA
LIMIT = 40 * 1024 * 1024


def exchange(partner, neighbours, fine_state):
    return pl.pallas_call(
        exchange_kernel,
        out_shape=(jax.ShapeDtypeStruct(PATCH, F32), jax.ShapeDtypeStruct((6, 5, *TILE), F32)),
        in_specs=[SMEM, SMEM, ANY],
        out_specs=(VMEM, VMEM),
        scratch_shapes=[
            pltpu.VMEM((6, *PATCH), F32),
            pltpu.VMEM((2, 5, 16, *TILE), F32),
            pltpu.VMEM((6, 5, *TILE), F32),
            pltpu.VMEM((32, 5, *TILE), F32),
            pltpu.VMEM((32, 5, *TILE), F32),
            DMA((8,)), DMA((32,)), DMA((32,)),
            DMA((2, PIECES)), DMA((2, PIECES)), DMA((2, PIECES)), DMA((2, PIECES)),
            DMA((2, HALF)), DMA((2, HALF)), DMA((2, HALF)), DMA((2, HALF)),
        ],
        compiler_params=pltpu.CompilerParams(collective_id=0, has_side_effects=True, vmem_limit_bytes=LIMIT),
        name="exchange",
    )(partner, neighbours, fine_state)


def fine_steps(partner, neighbours, work, link, migrated, ghosts, shape):
    return pl.pallas_call(
        fine_kernel,
        out_shape=(jax.ShapeDtypeStruct(shape, F32), jax.ShapeDtypeStruct((6, *TILE), F32)),
        in_specs=[SMEM, SMEM, SMEM, SMEM, ANY, VMEM],
        out_specs=(ANY, VMEM),
        scratch_shapes=[
            pltpu.VMEM((5, 34, *TILE), F32),
            pltpu.VMEM((10, 32, *TILE), F32),
            pltpu.VMEM((10, 32, *TILE), F32),
            pltpu.VMEM(PATCH, F32),
            pltpu.VMEM((5, *TILE), F32),
            pltpu.VMEM((40, 128), F32),
            DMA, DMA((8,)),
        ],
        compiler_params=pltpu.CompilerParams(vmem_limit_bytes=LIMIT),
        name="fine_steps",
    )(partner, neighbours, work, link, migrated, ghosts)


def coarse_step(message, coarse_state):
    return pl.pallas_call(
        coarse_kernel,
        out_shape=jax.ShapeDtypeStruct(coarse_state.shape, F32),
        in_specs=[VMEM, ANY],
        out_specs=ANY,
        scratch_shapes=[
            pltpu.VMEM((5, 34, *TILE), F32),
            pltpu.VMEM(PATCH, F32),
            pltpu.VMEM(PATCH, F32),
            pltpu.VMEM((2, 5, *TILE), F32),
            pltpu.VMEM((3, 6, *TILE), F32),
            pltpu.VMEM((6, 6, *TILE), F32),
            DMA((3,)), DMA((3,)), DMA((8,)),
        ],
        compiler_params=pltpu.CompilerParams(collective_id=1, has_side_effects=True, vmem_limit_bytes=LIMIT),
        name="coarse_step",
    )(message, coarse_state)


def body(fine_state, coarse_state, partner, mig_slot, neighbours, work, coarse_link):
    del mig_slot
    migrated, ghosts = exchange(partner, neighbours, fine_state)
    fine_out, message = fine_steps(partner, neighbours, work, coarse_link, migrated, ghosts, fine_state.shape)
    return fine_out, coarse_step(message, coarse_state)


def solution(mesh):
    return jax.shard_map(
        body,
        mesh=mesh,
        in_specs=(
            P("slab", "lvl", None, None, None),
            P("slab", "lvl", None, None, None),
            P(None, "lvl"),
            P(None, "lvl"),
            P(None, "lvl", None),
            P(None, "lvl"),
            P("slab", "lvl"),
        ),
        out_specs=(P("slab", "lvl", None, None, None), P("slab", "lvl", None, None, None)),
        check_vma=False,
    )
```

time: 686 us -> 88.8 us (0.13)
  waiting for transfers between devices: 357 us -> 0 us
  local copies, waits for them, and re-layouts: 184 us -> 3.35 us
  other arithmetic: 89.4 us -> 0 us
  Pallas kernels: 0 us -> 83.9 us
  between operations: 17.7 us -> 1.35 us
  matrix products: 14.7 us -> 0 us
  loops' own time: 10.1 us -> 0 us
  blocking collectives: 7.24 us -> 0 us
    all_gather x2 -> x0, waiting for transfers between devices: 194 us -> none  [the longest x1 138 us: body(): portion = lax.all_gather(outgoing, 'slab', axis=0, tiled=True)]
    unnamed x4 -> x0, waiting for transfers between devices: 162 us -> none
    pallas_call x0 -> x3, Pallas kernels: none -> 83.9 us  [the longest x1 42.1 us: exchange(): pl.pallas_call(exchange_kernel, out_shape=(jax.ShapeDtypeStruct(PATCH, F3...]
    scatter-add x5 -> x0, local copies, waits for them, and re-layouts: 34.2 us -> none  [the longest x3 26.5 us: apply_correction(): advanced = advanced.at[..., :, :, edge_index].add(amount)]
    slice x23 -> x0, local copies, waits for them, and re-layouts: 27.2 us -> none  [the longest x4 6.44 us: advance(): lax.index_in_dim(interface, faces_along - 1, spatial, keepdims=False)]
    another operation x16 -> x0, local copies, waits for them, and re-layouts: 27 us -> none  [the longest x8 10.3 us: face_layers(): jnp.stack([conserved[..., 0, :, :], conserved[..., -1, :, :], conserved[....]
    unnamed x83 -> x14, local copies, waits for them, and re-layouts: 29 us -> 3.35 us
    sub x7 -> x0, other arithmetic: 24 us -> none  [the longest x6 14.8 us: rusanov(): 0.5 * (flux_left + flux_right)]
  transfers between devices with their start and end apart: 3 -> 0, of which waited for: 3 -> 0; matrix products, arithmetic and copies ran while one was open for 11% -> 0% of each run, Pallas kernels for 0% -> 0%
where the time goes in v1:
time: 88.8 us; the launch traced here: 88.6 us
  Pallas kernels  83.9 us (94%)
  local copies, waits for them, and re-layouts  3.35 us (4%)
  between operations  1.35 us (2%)
    pallas_call x1, Pallas kernels, exchange(): pl.pallas_call(exchange_kernel, out_shape=(jax.ShapeDtypeStruct(PATCH, F3...  42.1 us
    pallas_call x1, Pallas kernels, fine_steps(): pl.pallas_call(fine_kernel, out_shape=(jax.ShapeDtypeStruct(shape, F32),...  30.4 us
    pallas_call x1, Pallas kernels, coarse_step(): pl.pallas_call(coarse_kernel, out_shape=jax.ShapeDtypeStruct(coarse_state...  11.5 us
    unnamed x14, local copies, waits for them, and re-layouts  3.35 us

profile of v1, /device:TPU:1, one launch (start us, length us, event | category | flops | bytes accessed | tf_op | source)
XLA Modules:
  0.0 88.6 jit_solution(1104042045713355637)
XLA Ops:
  0.6 0.0 copy-start.3
  1.3 0.0 copy-done.3
  1.3 0.0 copy-start.2
  1.3 0.1 copy.10.partner
  1.4 0.6 copy-done.2
  2.0 0.0 copy-start.4
  2.0 0.1 copy.11.neighbours
  2.1 0.6 copy-done.4
  2.7 0.1 copy.12.work
  2.7 0.0 copy-start
  2.7 1.1 %copy-done = f32[1,1,5,32,1024]{4,3,2,1,0:T(8,128)S(1)} copy-done((f32[1,1,5,32,1024]{4,3,2,1,0:T(8,128)S(1)}, f32[1,1,5,32,1024]{4,3,2,1,0:T(8,128)}, u32[]{:S(2)}) %copy-start) | copy-done | bytes 655384
  3.8 0.0 copy-start.1
  3.8 42.1 %exchange.1 = (f32[5,32,8,128]{3,2,1,0:T(8,128)S(1)}, f32[6,5,8,128]{3,2,1,0:T(8,128)S(1)}) custom-call(s32[32,1]{1,0:T(8,128)S(1)} %copy.10.partner, s32[32,1,6]{2,1,0:T(1,128)S(1)} %copy.11.neighbours, f32[1,1,5,32,1024]{4,3,2,1,0:T(8,128)S(1)} %copy-done), custom_call_target="tpu_custom_call" | custom-call | tf_op jit(solution)/shard_map/exchange/pallas_call | solution.py:506
  45.9 30.4 %fine_steps.1 = (f32[1,1,5,32,1024]{4,3,2,1,0:T(8,128)}, f32[6,8,128]{2,1,0:T(8,128)S(1)}) custom-call(s32[32,1]{1,0:T(8,128)S(1)} %copy.10.partner, s32[32,1,6]{2,1,0:T(1,128)S(1)} %copy.11.neighbours, s32[32,1]{1,0:T(8,128)S(1)} %copy.12.work, s32[1,1]{1,0:T(1,128)S(6)} %copy.14.link, f32[5,32,8,128]{3,2,1,0:T(8,128)S(1)} %get-tuple-element.6.migrated, ...), custom_call_target="tpu_custom_call" | custom-call | tf_op jit(solution)/shard_map/fine_steps/pallas_call | solution.py:527
  76.3 0.0 copy-done.1
  76.3 11.5 %coarse_step.1 = f32[1,1,5,32,1024]{4,3,2,1,0:T(8,128)S(1)} custom-call(f32[6,8,128]{2,1,0:T(8,128)S(1)} %get-tuple-element.9.message, f32[1,1,5,32,1024]{4,3,2,1,0:T(8,128)S(1)} %copy-done.1), custom_call_target="tpu_custom_call" | custom-call | tf_op jit(solution)/shard_map/coarse_step/pallas_call | solution.py:547
  87.8 0.8 copy.15
Async XLA Ops:
  0.6 0.7 copy-start.3
  1.3 0.7 copy-start.2
  2.0 0.7 copy-start.4
  2.7 1.1 %copy-start = (f32[1,1,5,32,1024]{4,3,2,1,0:T(8,128)S(1)}, f32[1,1,5,32,1024]{4,3,2,1,0:T(8,128)}, u32[]{:S(2)}) copy-start(f32[1,1,5,32,1024]{4,3,2,1,0:T(8,128)} %fine.1) | copy-start | bytes 1966084
  3.8 72.5 %copy-start.1 = (f32[1,1,5,32,1024]{4,3,2,1,0:T(8,128)S(1)}, f32[1,1,5,32,1024]{4,3,2,1,0:T(8,128)}, u32[]{:S(2)}) copy-start(f32[1,1,5,32,1024]{4,3,2,1,0:T(8,128)} %coarse.1) | copy-start | bytes 1966084

commit v2 on v1

--- a/solution.py
+++ b/solution.py
@@ -119,7 +119,7 @@
             state[f, x] = new[f]
         return (*after, above)
 
-    last = lax.fori_loop(1, 33, step, (*first, lowest))
+    last = lax.fori_loop(1, 33, step, (*first, lowest), unroll=4)
     return lowest, last[4]
 
 
@@ -188,7 +188,7 @@
             pack_z(own[f, x], x, side, carried[side * 5 + f]) for side in range(2) for f in range(5)
         )
 
-    packed = lax.fori_loop(0, 32, pack, (jnp.zeros(TILE, F32),) * 10)
+    packed = lax.fori_loop(0, 32, pack, (jnp.zeros(TILE, F32),) * 10, unroll=4)
     for side in range(2):
         for f in range(5):
             faces[4 + side, f] = packed[side * 5 + f]
@@ -280,7 +280,7 @@
             migrated[f, x] = held[chosen, f, x]
         return 0
 
-    lax.fori_loop(0, 32, choose, 0)
+    lax.fori_loop(0, 32, choose, 0, unroll=4)
 
 
 def fine_kernel(
@@ -322,7 +322,7 @@
                 outer[i, x] = v
         return 0
 
-    lax.fori_loop(0, 32, spread, 0)
+    lax.fori_loop(0, 32, spread, 0, unroll=4)
 
     for substep in range(4):
         active = substep < count
@@ -364,7 +364,7 @@
     def pack(x, carried):
         return tuple(pack_z(register[f, x], x, side, carried[f]) for f in range(5))
 
-    packed = lax.fori_loop(0, 32, pack, (jnp.zeros(TILE, F32),) * 5)
+    packed = lax.fori_loop(0, 32, pack, (jnp.zeros(TILE, F32),) * 5, unroll=4)
     flat = register.reshape(5 * 32 * 8, 128)
     source_lane = lax.broadcasted_iota(jnp.int32, (128, 128), 0)
     target_lane = lax.broadcasted_iota(jnp.int32, (128, 128), 1)
@@ -482,7 +482,7 @@
             state[f, x + 1] = cells[f]
         return 0
 
-    lax.fori_loop(0, 32, correct, 0)
+    lax.fori_loop(0, 32, correct, 0, unroll=4)
     stores = [
         pltpu.make_async_copy(
             state.at[:, pl.ds(1, 32), j, :], out.at[0, 0, :, :, pl.ds(j * 128, 128)], sem.at[j]

time: 88.8 us -> 65.7 us (0.74)
  Pallas kernels: 83.9 us -> 60.8 us
    pallas_call x1, Pallas kernels: 30.4 us -> 13.4 us  [fine_steps(): pl.pallas_call(fine_kernel, out_shape=(jax.ShapeDtypeStruct(shape, F32),...]
    pallas_call x1, Pallas kernels: 11.5 us -> 6.99 us  [coarse_step(): pl.pallas_call(coarse_kernel, out_shape=jax.ShapeDtypeStruct(coarse_state...]
    pallas_call x1, Pallas kernels: 42.1 us -> 40.4 us  [exchange(): pl.pallas_call(exchange_kernel, out_shape=(jax.ShapeDtypeStruct(PATCH, F3...]
where the time goes in v2:
time: 65.7 us; the launch traced here: 65.5 us
  Pallas kernels  60.8 us (93%)
  local copies, waits for them, and re-layouts  3.35 us (5%)
  between operations  1.35 us (2%)
    pallas_call x1, Pallas kernels, exchange(): pl.pallas_call(exchange_kernel, out_shape=(jax.ShapeDtypeStruct(PATCH, F3...  40.4 us
    pallas_call x1, Pallas kernels, fine_steps(): pl.pallas_call(fine_kernel, out_shape=(jax.ShapeDtypeStruct(shape, F32),...  13.4 us
    pallas_call x1, Pallas kernels, coarse_step(): pl.pallas_call(coarse_kernel, out_shape=jax.ShapeDtypeStruct(coarse_state...  6.99 us
    unnamed x14, local copies, waits for them, and re-layouts  3.35 us

profile of v2, /device:TPU:1, one launch (start us, length us, event | category | flops | bytes accessed | tf_op | source)
XLA Modules:
  0.0 65.5 jit_solution(12010424413876214239)
XLA Ops:
  0.6 0.0 copy-start.3
  1.3 0.0 copy-done.3
  1.3 0.0 copy-start.2
  1.3 0.1 copy.10.partner
  1.4 0.6 copy-done.2
  2.0 0.0 copy-start.4
  2.0 0.1 copy.11.neighbours
  2.1 0.6 copy-done.4
  2.7 0.1 copy.12.work
  2.7 0.0 copy-start
  2.7 1.1 %copy-done = f32[1,1,5,32,1024]{4,3,2,1,0:T(8,128)S(1)} copy-done((f32[1,1,5,32,1024]{4,3,2,1,0:T(8,128)S(1)}, f32[1,1,5,32,1024]{4,3,2,1,0:T(8,128)}, u32[]{:S(2)}) %copy-start) | copy-done | bytes 655384
  3.8 0.0 copy-start.1
  3.8 40.4 %exchange.1 = (f32[5,32,8,128]{3,2,1,0:T(8,128)S(1)}, f32[6,5,8,128]{3,2,1,0:T(8,128)S(1)}) custom-call(s32[32,1]{1,0:T(8,128)S(1)} %copy.10.partner, s32[32,1,6]{2,1,0:T(1,128)S(1)} %copy.11.neighbours, f32[1,1,5,32,1024]{4,3,2,1,0:T(8,128)S(1)} %copy-done), custom_call_target="tpu_custom_call" | custom-call | tf_op jit(solution)/shard_map/exchange/pallas_call | solution.py:506
  44.2 13.4 %fine_steps.1 = (f32[1,1,5,32,1024]{4,3,2,1,0:T(8,128)}, f32[6,8,128]{2,1,0:T(8,128)S(1)}) custom-call(s32[32,1]{1,0:T(8,128)S(1)} %copy.10.partner, s32[32,1,6]{2,1,0:T(1,128)S(1)} %copy.11.neighbours, s32[32,1]{1,0:T(8,128)S(1)} %copy.12.work, s32[1,1]{1,0:T(1,128)S(6)} %copy.14.link, f32[5,32,8,128]{3,2,1,0:T(8,128)S(1)} %get-tuple-element.6.migrated, ...), custom_call_target="tpu_custom_call" | custom-call | tf_op jit(solution)/shard_map/fine_steps/pallas_call | solution.py:527
  57.6 0.0 copy-done.1
  57.6 7.0 %coarse_step.1 = f32[1,1,5,32,1024]{4,3,2,1,0:T(8,128)S(1)} custom-call(f32[6,8,128]{2,1,0:T(8,128)S(1)} %get-tuple-element.9.message, f32[1,1,5,32,1024]{4,3,2,1,0:T(8,128)S(1)} %copy-done.1), custom_call_target="tpu_custom_call" | custom-call | tf_op jit(solution)/shard_map/coarse_step/pallas_call | solution.py:547
  64.6 0.8 %copy.15 = f32[1,1,5,32,1024]{4,3,2,1,0:T(8,128)} copy(f32[1,1,5,32,1024]{4,3,2,1,0:T(8,128)S(1)} %coarse_step.1) | data formatting | bytes 1310720
Async XLA Ops:
  0.6 0.7 %copy-start.3 = (s32[32,1]{0,1:T(1,128)S(1)}, s32[32,1]{0,1:T(1,128)}, u32[]{:S(2)}) copy-start(s32[32,1]{0,1:T(1,128)} %param.9) | copy-start | bytes 388
  1.3 0.7 %copy-start.2 = (s32[32,1,6]{0,1,2:T(1,128)S(1)}, s32[32,1,6]{0,1,2:T(1,128)}, u32[]{:S(2)}) copy-start(s32[32,1,6]{0,1,2:T(1,128)} %param.10) | copy-start | bytes 2308
  2.0 0.7 %copy-start.4 = (s32[32,1]{0,1:T(1,128)S(1)}, s32[32,1]{0,1:T(1,128)}, u32[]{:S(2)}) copy-start(s32[32,1]{0,1:T(1,128)} %param.11) | copy-start | bytes 388
  2.7 1.1 %copy-start = (f32[1,1,5,32,1024]{4,3,2,1,0:T(8,128)S(1)}, f32[1,1,5,32,1024]{4,3,2,1,0:T(8,128)}, u32[]{:S(2)}) copy-start(f32[1,1,5,32,1024]{4,3,2,1,0:T(8,128)} %fine.1) | copy-start | bytes 1966084
  3.8 53.8 %copy-start.1 = (f32[1,1,5,32,1024]{4,3,2,1,0:T(8,128)S(1)}, f32[1,1,5,32,1024]{4,3,2,1,0:T(8,128)}, u32[]{:S(2)}) copy-start(f32[1,1,5,32,1024]{4,3,2,1,0:T(8,128)} %coarse.1) | copy-start | bytes 1966084

commit v3 on v2

v3 whole, which is shorter than its diff:
```python
import jax
import jax.numpy as jnp
from jax import lax
from jax.experimental import pallas as pl
from jax.experimental.pallas import tpu as pltpu
from jax.sharding import PartitionSpec as P

MESH = pl.DeviceIdType.MESH
F32 = jnp.float32
COARSE_STEP = 0.035
TILE = (8, 128)
PATCH = (5, 32, 8, 128)
CHUNK = 4
CHUNKS = 32 // CHUNK
NOTE = CHUNKS
PLANES = 35
ORDER = (0, 1, 2, 3, 4, 5, NOTE, 6, 7)


def lanes():
    return lax.broadcasted_iota(jnp.int32, TILE, 1)


def rows():
    return lax.broadcasted_iota(jnp.int32, TILE, 0)


def primitives(cells):
    density, mom_x, mom_y, mom_z, energy = cells
    inverse = 1.0 / density
    vel = [mom_x * inverse, mom_y * inverse, mom_z * inverse]
    kinetic = 0.5 * (mom_x * vel[0] + mom_y * vel[1] + mom_z * vel[2])
    pressure = 0.4 * (energy - kinetic)
    half_sound = 0.5 * jnp.sqrt(1.4 * pressure * inverse)
    return (*vel, pressure, half_sound)


def half_flux(cells, prims, direction):
    half_normal = 0.5 * prims[direction]
    pressure, half_sound = prims[3], prims[4]
    flux = [cells[1 + i] * half_normal for i in range(3)]
    flux[direction] = flux[direction] + 0.5 * pressure
    flux.append((cells[4] + pressure) * half_normal)
    return flux, jnp.abs(half_normal) + half_sound


def interface(low, low_flux, low_speed, high, high_flux, high_speed, direction, sign=None):
    fastest = jnp.maximum(low_speed, high_speed)
    if sign is not None:
        fastest = fastest * sign
    out = [0.5 * (low[1 + direction] + high[1 + direction]) - fastest * (high[0] - low[0])]
    for i in range(4):
        out.append((low_flux[i] + high_flux[i]) - fastest * (high[1 + i] - low[1 + i]))
    return out


def z_up(v):
    return pltpu.roll(v, 127, 1)


def z_down(v):
    return pltpu.roll(v, 1, 1)


def y_up(v):
    return pltpu.roll(jnp.where(lanes() < 32, pltpu.roll(v, 7, 0), v), 96, 1)


def y_down(v):
    return pltpu.roll(jnp.where(lanes() >= 96, pltpu.roll(v, 1, 0), v), 32, 1)


def edge_masks(direction):
    if direction == 1:
        return (rows() == 0) & (lanes() < 32), (rows() == 7) & (lanes() >= 96)
    return lanes() % 32 == 0, lanes() % 32 == 31


def face_sign(direction):
    lower = rows() < 4 if direction == 1 else lanes() % 32 < 16
    return jnp.where(lower, -1.0, 1.0).astype(F32)


def across(cells, prims, direction, outer):
    up, down = (y_up, y_down) if direction == 1 else (z_up, z_down)
    flux, speed = half_flux(cells, prims, direction)
    inner = interface(
        cells, flux, speed, [up(v) for v in cells], [up(v) for v in flux], up(speed), direction
    )
    border = outer(flux, speed)
    lower, upper = edge_masks(direction)
    change = [
        jnp.where(upper, border[i], inner[i]) - jnp.where(lower, border[i], down(inner[i])) for i in range(5)
    ]
    return change, border


def load_plane(ref, x):
    return [ref[f, x] for f in range(5)]


def prepare(state, x):
    cells = load_plane(state, x)
    prims = primitives(cells)
    flux, speed = half_flux(cells, prims, 0)
    return cells, prims, flux, speed


def lowest_interface(state):
    ghost, _, ghost_flux, ghost_speed = prepare(state, 0)
    first, _, flux, speed = prepare(state, 1)
    return interface(ghost, ghost_flux, ghost_speed, first, flux, speed, 0)


def advance(state, first, count, below, update):
    cells, prims, flux, speed = prepare(state, first)
    for n in range(count):
        after = prepare(state, first + n + 1)
        above = interface(cells, flux, speed, after[0], after[2], after[3], 0)
        new = update(first + n - 1, cells, prims, [above[i] - below[i] for i in range(5)])
        for f in range(5):
            state[f, first + n] = new[f]
        cells, prims, flux, speed = after
        below = above
    return below


def pack_y(flat, first, side):
    out = None
    for g in range(4):
        part = flat[pl.ds(first + g * 8 + 7 * side, 8, stride=32), :]
        part = pltpu.roll(part, (32 * g - 96 * side) % 128, 1)
        out = part if g == 0 else jnp.where(lanes() // 32 == g, part, out)
    return out


def pack_z(plane, x, side, out):
    return jnp.where(lanes() % 32 == x, pltpu.roll(plane, (x + 128 - 31 * side) % 128, 1), out)


def pack_z_faces(ref, first):
    def pack(x, carried):
        return tuple(
            pack_z(ref[f, first + x], x, side, carried[side * 5 + f]) for side in range(2) for f in range(5)
        )

    return lax.fori_loop(0, 32, pack, (jnp.zeros(TILE, F32),) * 10, unroll=4)


def spread_y(face, field, x, side):
    row = jnp.broadcast_to(face[field, pl.ds(x // 4, 1), :], TILE)
    shift = (3 - x % 4) * 32 if side else (4 - x % 4) * 32
    return pltpu.roll(row, shift % 128, 1)


def spread_z(face, field, x, side):
    return pltpu.roll(face[field], (128 - x + 31 * side) % 128, 1)


def step_kernel(
    partner, neighbours, work, link, fine, coarse, fine_result, coarse_result,
    held, relay, faces, messages, landed, ghosts, marks,
    outer_y, outer_z, register, x_register, carry, squeezed,
    coarse_state, flux_y, flux_z, flux_x, note, notes, totals,
    load_sem, coarse_sem, ghost_send, ghost_recv, mark_send, mark_recv, note_send, note_recv,
    near_send, near_recv, far_send, far_recv, up_send, up_recv, on_send, on_recv,
):
    slab = lax.axis_index("slab")
    lvl = lax.axis_index("lvl")
    other_lvl = lvl ^ 2
    own = held.at[0]

    def loads_of(source, target, sem):
        return [
            pltpu.make_async_copy(
                source.at[0, 0, :, :, pl.ds(j * 128, 128)], target.at[:, pl.ds(1, 32), j, :], sem.at[j]
            )
            for j in range(8)
        ]

    fine_loads = loads_of(fine, own, load_sem)
    coarse_loads = loads_of(coarse, coarse_state, coarse_sem)
    for copy in fine_loads + coarse_loads:
        copy.start()

    barrier = pltpu.get_barrier_semaphore()
    greeted = [(slab ^ turn, lvl) for turn in range(1, 32)]
    greeted += [(slab, lvl ^ turn) for turn in range(1, 4)] + [(slab ^ 16, other_lvl)]
    for device in greeted:
        pl.semaphore_signal(barrier, inc=1, device_id=device, device_id_type=MESH)

    code = link[0, 0]
    valid = code >= 0
    level = jnp.maximum(code, 0) // 24
    face = jnp.maximum(code, 0) % 24 // 4
    quarter = jnp.maximum(code, 0) % 4
    marks[0] = jnp.full(TILE, face.astype(F32), F32)
    apart = partner[0, slab] ^ slab
    chosen = jnp.int32(0)
    for bit in range(5):
        chosen = chosen + (apart >= (1 << bit)).astype(jnp.int32)

    def choose(values):
        out = values[0]
        for n in range(1, 6):
            out = jnp.where(chosen == n, values[n], out)
        return out

    for copy in fine_loads:
        copy.wait()
    flat = own.reshape(5 * PLANES * 8, 128)
    for f in range(5):
        faces[0, f] = own[f, 1]
        faces[1, f] = own[f, 32]
        for side in range(2):
            faces[2 + side, f] = pack_y(flat, (f * PLANES + 1) * 8, side)
    packed = pack_z_faces(own, 1)
    for side in range(2):
        for f in range(5):
            faces[4 + side, f] = packed[side * 5 + f]

    pl.semaphore_wait(barrier, len(greeted))

    linked = [neighbours[f, 0, slab] for f in range(6)]
    ghost_copies = []
    for turn in range(1, 32):
        there = slab ^ turn
        which = jnp.int32(0)
        for f in range(1, 6):
            which = jnp.where(linked[f] == there, f, which)
        for f in range(5):
            messages[turn, f] = faces[which, f]
        copy = pltpu.make_async_remote_copy(
            src_ref=messages.at[turn], dst_ref=landed.at[turn],
            send_sem=ghost_send.at[turn], recv_sem=ghost_recv.at[turn],
            device_id=(there, lvl), device_id_type=MESH,
        )
        copy.start()
        ghost_copies.append(copy)
    mark_copies = []
    for bit in range(5):
        copy = pltpu.make_async_remote_copy(
            src_ref=marks.at[0], dst_ref=marks.at[1 + bit],
            send_sem=mark_send.at[bit], recv_sem=mark_recv.at[bit],
            device_id=(slab ^ (1 << bit), lvl), device_id_type=MESH,
        )
        copy.start()
        mark_copies.append(copy)

    for copy in coarse_loads:
        copy.wait()
    for f in range(5):
        coarse_state[f, 0] = coarse_state[f, 1]
        coarse_state[f, 33] = coarse_state[f, 32]

    def coarse_update(x, cells, prims, change):
        for d, kept in ((1, flux_y), (2, flux_z)):

            def border(flux, speed, d=d):
                return [cells[1 + d]] + [2.0 * v for v in flux]

            part, values = across(cells, prims, d, border)
            change = [change[i] + part[i] for i in range(5)]
            for i in range(5):
                kept[i, x] = values[i]
        return [cells[i] - COARSE_STEP * change[i] for i in range(5)]

    lowest = lowest_interface(coarse_state)

    def coarse_chunk(c, below):
        return tuple(advance(coarse_state, 1 + c * CHUNK, CHUNK, below, coarse_update))

    highest = lax.fori_loop(0, CHUNKS, coarse_chunk, tuple(lowest))
    for i in range(5):
        flux_x[0, i] = lowest[i]
        flux_x[1, i] = highest[i]

    for copy in ghost_copies + mark_copies:
        copy.wait_recv()
    present = [linked[f] >= 0 for f in range(6)]
    for f in range(6):
        turn = jnp.maximum(linked[f], 0) ^ slab
        for i in range(5):
            ghosts[f, i] = landed[turn, i]
    for f in range(5):
        own[f, 0] = jnp.where(present[0], ghosts[0, f], own[f, 1])
        own[f, 33] = jnp.where(present[1], ghosts[1, f], own[f, 32])
    mark = choose([marks[n] for n in range(6)])
    along_y = (mark == 2.0) | (mark == 3.0)

    count = work[0, slab]
    steps = jnp.full(TILE, count.astype(F32), F32)
    ratio = 2.0 * COARSE_STEP / steps
    share = 1.0 / steps

    def spread(x):
        cells = load_plane(own, x + 1)
        for d, spreader, outer in ((1, spread_y, outer_y), (2, spread_z, outer_z)):
            lower = rows() < 4 if d == 1 else lanes() % 32 < 16
            values = []
            for f in range(5):
                low = jnp.where(present[2 * d], spreader(ghosts.at[2 * d], f, x, 0), cells[f])
                high = jnp.where(present[2 * d + 1], spreader(ghosts.at[2 * d + 1], f, x, 1), cells[f])
                values.append(jnp.where(lower, low, high))
            flux, speed = half_flux(values, primitives(values), d)
            for i, v in enumerate(values + flux + [speed]):
                outer[i, x] = v

    def updater(substep):
        active = substep < count

        def update(x, cells, prims, change):
            borders = []
            for d, outer in ((1, outer_y), (2, outer_z)):

                def border(flux, speed, d=d, outer=outer):
                    return interface(
                        cells, flux, speed, [outer[i, x] for i in range(5)],
                        [outer[5 + i, x] for i in range(4)], outer[9, x], d, face_sign(d),
                    )

                part, values = across(cells, prims, d, border)
                borders.append(values)
                change = [change[i] + part[i] for i in range(5)]
            for i in range(5):
                value = jnp.where(along_y, borders[0][i], borders[1][i])
                value = jnp.where(active, value * share, 0.0)
                register[i, x] = value if substep == 0 else register[i, x] + value
            return [jnp.where(active, cells[i] - ratio * change[i], cells[i]) for i in range(5)]

        return update

    def outermost(substep, side, values):
        for i in range(5):
            value = jnp.where(substep < count, values[i] * share, 0.0)
            x_register[side, i] = value if substep == 0 else x_register[side, i] + value

    def span(ref, piece):
        if isinstance(piece, int) and piece == NOTE:
            return ref.at[:, pl.ds(34, 1)]
        return ref.at[:, pl.ds(1 + piece * CHUNK, CHUNK)]

    def near(axis, piece):
        return pltpu.make_async_remote_copy(
            src_ref=span(own, piece), dst_ref=span(held.at[1 + 2 * axis], piece),
            send_sem=near_send.at[axis, piece], recv_sem=near_recv.at[axis, piece],
            device_id=(slab ^ (4 if axis else 1), lvl), device_id_type=MESH,
        )

    def far(axis, piece):
        return pltpu.make_async_remote_copy(
            src_ref=span(held.at[1 + 2 * axis], piece), dst_ref=span(held.at[2 + 2 * axis], piece),
            send_sem=far_send.at[axis, piece], recv_sem=far_recv.at[axis, piece],
            device_id=(slab ^ (12 if axis else 3), lvl), device_id_type=MESH,
        )

    def up(piece):
        return pltpu.make_async_remote_copy(
            src_ref=span(own, piece), dst_ref=span(relay, piece),
            send_sem=up_send.at[piece], recv_sem=up_recv.at[piece],
            device_id=(slab ^ (piece % 2 * 16), other_lvl), device_id_type=MESH,
        )

    def on(piece):
        return pltpu.make_async_remote_copy(
            src_ref=span(relay, piece), dst_ref=span(held.at[5], piece),
            send_sem=on_send.at[piece], recv_sem=on_recv.at[piece],
            device_id=(slab ^ ((piece + 1) % 2 * 16), other_lvl), device_id_type=MESH,
        )

    def send(piece):
        near(0, piece).start()
        near(1, piece).start()
        up(piece).start()

    def forward(piece):
        for axis in range(2):
            near(axis, piece).wait_recv()
            far(axis, piece).start()
        up(piece).wait_recv()
        on(piece).start()

    def arrive(piece):
        far(0, piece).wait_recv()
        far(1, piece).wait_recv()
        on(piece).wait_recv()

    for x in range(3):
        spread(x)
    for substep in range(4):
        lowest = lowest_interface(own)
        outermost(substep, 0, lowest)
        below = advance(own, 1, 3 - substep, lowest, updater(substep)) if substep < 3 else lowest
        for i in range(5):
            carry[substep, i] = below[i]

    def wave(c, _):
        for n in range(CHUNK):
            spread(c * CHUNK - 1 + n)
        for substep in range(4):
            below = [carry[substep, i] for i in range(5)]
            below = advance(own, c * CHUNK - substep, CHUNK, below, updater(substep))
            for i in range(5):
                carry[substep, i] = below[i]

        @pl.when(c < 7)
        def _():
            send(c - 1)

        @pl.when((c == 4) | (c == 6))
        def _():
            forward(c // 2 - 2)

        return 0

    lax.fori_loop(1, CHUNKS, wave, 0)
    spread(31)
    for substep in range(4):
        below = [carry[substep, i] for i in range(5)]
        outermost(substep, 1, advance(own, 32 - substep, substep + 1, below, updater(substep)))
    forward(2)

    packed = pack_z_faces(register, 0)
    flat = register.reshape(5 * 32 * 8, 128)
    source_lane = lax.broadcasted_iota(jnp.int32, (128, 128), 0)
    target_lane = lax.broadcasted_iota(jnp.int32, (128, 128), 1)
    wanted = target_lane // 32 * 64 + target_lane % 32 * 2
    squeeze = ((source_lane == wanted) & (target_lane % 32 < 16) & (target_lane < 64)).astype(F32)
    for f in range(5):
        options = [x_register[0, f], x_register[1, f], pack_y(flat, f * 256, 0), pack_y(flat, f * 256, 1)]
        value = packed[5 + f]
        for n, option in enumerate([*options, packed[f]]):
            value = jnp.where(mark == float(n), option, value)
        value = value + pltpu.roll(value, 127, 1)
        value = 0.25 * (value + pltpu.roll(value, 96, 1))
        squeezed[pl.ds(f * 8, 8), :] = jnp.dot(
            value, squeeze, precision=lax.Precision.HIGHEST, preferred_element_type=F32
        )
    low_lanes = lax.broadcasted_iota(jnp.int32, (4, 128), 1) < 64
    for f in range(5):
        even = squeezed[pl.ds(f * 8, 4, stride=2), :]
        odd = squeezed[pl.ds(f * 8 + 1, 4, stride=2), :]
        own[f, 34, pl.ds(0, 4), :] = jnp.where(low_lanes, even, pltpu.roll(odd, 64, 1))
        own[f, 34, pl.ds(4, 4), :] = jnp.zeros((4, 128), F32)

    for piece in ORDER[6:]:
        send(piece)

    direction = face // 2
    quarter_row = jnp.where(direction == 2, quarter % 2, quarter // 2)
    quarter_col = jnp.where(direction == 2, quarter // 2, quarter % 2)
    note_copies = [
        pltpu.make_async_remote_copy(
            src_ref=note, dst_ref=notes.at[turn - 1],
            send_sem=note_send.at[turn - 1], recv_sem=note_recv.at[turn - 1],
            device_id=(slab, lvl ^ turn), device_id_type=MESH,
        )
        for turn in range(1, 4)
    ]

    def take(piece):
        arrive(piece)
        if piece != NOTE:
            for n in range(CHUNK):
                x = piece * CHUNK + n
                for f in range(5):
                    fine_result[f, x] = choose([held[k, f, x + 1] for k in range(6)])
            return
        for f in range(5):
            small = choose([held[k, f, 34, pl.ds(0, 4), :] for k in range(6)])
            small = jnp.where(quarter_col == 0, small, pltpu.roll(small, 16, 1))
            note[f, pl.ds(0, 4), :] = jnp.where(quarter_row == 0, small, 0.0)
            note[f, pl.ds(4, 4), :] = jnp.where(quarter_row == 1, small, 0.0)
        place = level * 6 + (face ^ 1) + 1
        inside = (rows() // 4 == quarter_row) & (lanes() % 32 // 16 == quarter_col)
        note[5] = jnp.where(inside & valid, place.astype(F32), 0.0)
        for copy in note_copies:
            copy.start()

    for piece in range(3, 6):
        forward(piece)
        take(piece - 3)
    forward(NOTE)
    take(3)
    forward(6)
    take(4)
    take(5)
    take(NOTE)
    forward(7)
    take(6)

    for copy in note_copies:
        copy.wait_recv()
    for g in range(6):
        key = (lvl * 6 + g + 1).astype(F32)
        parts = [note if n == 3 else notes.at[n] for n in range(4)]
        hits = [part[5] == key for part in parts]
        for f in range(5):
            total = jnp.zeros(TILE, F32)
            for n in range(4):
                total = total + jnp.where(hits[n], parts[n][f], 0.0)
            totals[g, f] = total
        cover = jnp.zeros(TILE, F32)
        for n in range(4):
            cover = cover + jnp.where(hits[n], 1.0, 0.0)
        totals[g, 5] = cover

    for side, x in ((0, 1), (1, 32)):
        for f in range(5):
            amount = totals[side, 5] * flux_x[side, f] - totals[side, f]
            coarse_state[f, x] = coarse_state[f, x] + (COARSE_STEP if side else -COARSE_STEP) * amount

    def correct(x, _):
        cells = load_plane(coarse_state, x + 1)
        for d, spreader, kept in ((1, spread_y, flux_y), (2, spread_z, flux_z)):
            lower, upper = edge_masks(d)
            weight = COARSE_STEP * face_sign(d) * (lower | upper).astype(F32)

            def both(f, d=d, spreader=spreader, upper=upper):
                low = spreader(totals.at[2 * d], f, x, 0)
                high = spreader(totals.at[2 * d + 1], f, x, 1)
                return jnp.where(upper, high, low)

            cover = both(5)
            for f in range(5):
                cells[f] = cells[f] + weight * (cover * kept[f, x] - both(f))
        for f in range(5):
            coarse_result[f, x] = cells[f]
        return 0

    lax.fori_loop(0, 32, correct, 0, unroll=4)
    take(7)

    for copy in ghost_copies + mark_copies + note_copies:
        copy.wait_send()
    for piece in range(CHUNKS + 1):
        for axis in range(2):
            near(axis, piece).wait_send()
            far(axis, piece).wait_send()
        up(piece).wait_send()
        on(piece).wait_send()


def write_kernel(fine_result, coarse_result, fine_out, coarse_out, sem):
    copies = [
        pltpu.make_async_copy(
            source.at[:, :, j, :], target.at[0, 0, :, :, pl.ds(j * 128, 128)], sem.at[n, j]
        )
        for n, (source, target) in enumerate(((fine_result, fine_out), (coarse_result, coarse_out)))
        for j in range(8)
    ]
    for copy in copies:
        copy.start()
    for copy in copies:
        copy.wait()


SMEM = pl.BlockSpec(memory_space=pltpu.SMEM)
VMEM = pl.BlockSpec(memory_space=pltpu.VMEM)
HBM = pl.BlockSpec(memory_space=pltpu.HBM)
DMA = pltpu.SemaphoreType.DMA
LIMIT = 40 * 1024 * 1024


def step(partner, neighbours, work, link, fine_state, coarse_state):
    pieces = CHUNKS + 1
    return pl.pallas_call(
        step_kernel,
        out_shape=(jax.ShapeDtypeStruct(PATCH, F32), jax.ShapeDtypeStruct(PATCH, F32)),
        in_specs=[SMEM, SMEM, SMEM, SMEM, HBM, HBM],
        out_specs=(VMEM, VMEM),
        scratch_shapes=[
            pltpu.VMEM((6, 5, PLANES, *TILE), F32),
            pltpu.VMEM((5, PLANES, *TILE), F32),
            pltpu.VMEM((6, 5, *TILE), F32),
            pltpu.VMEM((32, 5, *TILE), F32),
            pltpu.VMEM((32, 5, *TILE), F32),
            pltpu.VMEM((6, 5, *TILE), F32),
            pltpu.VMEM((6, *TILE), F32),
            pltpu.VMEM((10, 32, *TILE), F32),
            pltpu.VMEM((10, 32, *TILE), F32),
            pltpu.VMEM(PATCH, F32),
            pltpu.VMEM((2, 5, *TILE), F32),
            pltpu.VMEM((4, 5, *TILE), F32),
            pltpu.VMEM((40, 128), F32),
            pltpu.VMEM((5, 34, *TILE), F32),
            pltpu.VMEM(PATCH, F32),
            pltpu.VMEM(PATCH, F32),
            pltpu.VMEM((2, 5, *TILE), F32),
            pltpu.VMEM((6, *TILE), F32),
            pltpu.VMEM((3, 6, *TILE), F32),
            pltpu.VMEM((6, 6, *TILE), F32),
            DMA((8,)), DMA((8,)), DMA((32,)), DMA((32,)), DMA((5,)), DMA((5,)), DMA((3,)), DMA((3,)),
            DMA((2, pieces)), DMA((2, pieces)), DMA((2, pieces)), DMA((2, pieces)),
            DMA((pieces,)), DMA((pieces,)), DMA((pieces,)), DMA((pieces,)),
        ],
        compiler_params=pltpu.CompilerParams(collective_id=0, has_side_effects=True, vmem_limit_bytes=LIMIT),
        name="step",
    )(partner, neighbours, work, link, fine_state, coarse_state)


def write(fine_result, coarse_result, shape):
    return pl.pallas_call(
        write_kernel,
        out_shape=(jax.ShapeDtypeStruct(shape, F32),) * 2,
        in_specs=[VMEM, VMEM],
        out_specs=(HBM, HBM),
        scratch_shapes=[DMA((2, 8))],
        name="write",
    )(fine_result, coarse_result)


def body(fine_state, coarse_state, partner, mig_slot, neighbours, work, coarse_link):
    del mig_slot
    results = step(
        partner.T, jnp.transpose(neighbours, (2, 1, 0)), work.T, coarse_link, fine_state, coarse_state
    )
    return write(*results, fine_state.shape)


def solution(mesh):
    return jax.shard_map(
        body,
        mesh=mesh,
        in_specs=(
            P("slab", "lvl", None, None, None),
            P("slab", "lvl", None, None, None),
            P(None, "lvl"),
            P(None, "lvl"),
            P(None, "lvl", None),
            P(None, "lvl"),
            P("slab", "lvl"),
        ),
        out_specs=(P("slab", "lvl", None, None, None), P("slab", "lvl", None, None, None)),
        check_vma=False,
    )
```

time: 65.7 us -> 61.2 us (0.932)
  Pallas kernels: 60.8 us -> 55.1 us
  local copies, waits for them, and re-layouts: 3.35 us -> 4.51 us
    pallas_call x3 -> x2, Pallas kernels: 60.8 us -> 55.1 us  [the longest x1 52.7 us: step(): pl.pallas_call(step_kernel, out_shape=(jax.ShapeDtypeStruct(PATCH, F32),...]
    unnamed x14, local copies, waits for them, and re-layouts: 3.35 us -> 4.51 us
where the time goes in v3:
time: 61.2 us; the launch traced here: 61 us
  Pallas kernels  55.1 us (90%)
  local copies, waits for them, and re-layouts  4.51 us (7%)
  between operations  1.32 us (2%)
    pallas_call x1, Pallas kernels, step(): pl.pallas_call(step_kernel, out_shape=(jax.ShapeDtypeStruct(PATCH, F32),...  52.7 us
    unnamed x14, local copies, waits for them, and re-layouts  4.51 us
    pallas_call x1, Pallas kernels, write(): pl.pallas_call(write_kernel, out_shape=(jax.ShapeDtypeStruct(shape, F32),...  2.46 us

profile of v3, /device:TPU:1, one launch (start us, length us, event | category | flops | bytes accessed | tf_op | source)
XLA Modules:
  0.0 61.0 jit_solution(13539400838165965940)
XLA Ops:
  1.3 0.0 copy-start.4
  1.3 0.0 copy-start.5
  1.3 0.0 copy-start.6
  1.3 0.7 %copy-done.4 = s32[32,1,6]{0,1,2:T(1,128)S(1)} copy-done((s32[32,1,6]{0,1,2:T(1,128)S(1)}, s32[32,1,6]{0,1,2:T(1,128)}, u32[]{:S(2)}) %copy-start.4) | copy-done | bytes 792
  2.0 0.0 copy-done.5
  2.0 0.0 copy-done.6
  2.0 0.0 copy-start
  2.0 1.1 %copy-done = f32[1,1,5,32,1024]{4,3,2,1,0:T(8,128)S(1)} copy-done((f32[1,1,5,32,1024]{4,3,2,1,0:T(8,128)S(1)}, f32[1,1,5,32,1024]{4,3,2,1,0:T(8,128)}, u32[]{:S(2)}) %copy-start) | copy-done | bytes 655384
  3.1 0.0 copy-start.1
  3.1 1.1 %copy-done.1 = f32[1,1,5,32,1024]{4,3,2,1,0:T(8,128)S(1)} copy-done((f32[1,1,5,32,1024]{4,3,2,1,0:T(8,128)S(1)}, f32[1,1,5,32,1024]{4,3,2,1,0:T(8,128)}, u32[]{:S(2)}) %copy-start.1) | copy-done | bytes 655384
  4.1 52.7 %step.1 = (f32[5,32,8,128]{3,2,1,0:T(8,128)S(1)}, f32[5,32,8,128]{3,2,1,0:T(8,128)S(1)}) custom-call(s32[1,32]{1,0:T(1,128)S(1)} %bitcast.4, s32[6,1,32]{2,1,0:T(1,128)S(1)} %bitcast.3, s32[1,32]{1,0:T(1,128)S(1)} %bitcast.5, s32[1,1]{1,0:T(1,128)S(6)} %copy.8.link, f32[1,1,5,32,1024]{4,3,2,1,0:T(8,128)S(1)} %copy-done, f32[1,1,5,32,1024]{4,3,2,1,0:T(8,128)S(1)} %copy-done.1), custom_call_target="tpu_custom_call" | custom-call | tf_op jit(solution)/shard_map/step/pallas_call | solution.py:567
  56.8 0.0 copy-start.2
  56.8 0.8 %copy-done.2 = f32[5,32,8,128]{3,2,1,0:T(8,128)} copy-done((f32[5,32,8,128]{3,2,1,0:T(8,128)}, f32[5,32,8,128]{3,2,1,0:T(8,128)S(1)}, u32[]{:S(2)}) %copy-start.2) | copy-done | bytes 655384
  57.7 0.0 copy-start.3
  57.7 0.8 %copy-done.3 = f32[5,32,8,128]{3,2,1,0:T(8,128)} copy-done((f32[5,32,8,128]{3,2,1,0:T(8,128)}, f32[5,32,8,128]{3,2,1,0:T(8,128)S(1)}, u32[]{:S(2)}) %copy-start.3) | copy-done | bytes 655384
  58.5 2.5 %write.1 = (f32[1,1,5,32,1024]{4,3,2,1,0:T(8,128)}, f32[1,1,5,32,1024]{4,3,2,1,0:T(8,128)}) custom-call(f32[5,32,8,128]{3,2,1,0:T(8,128)} %copy-done.2, f32[5,32,8,128]{3,2,1,0:T(8,128)} %copy-done.3), custom_call_target="tpu_custom_call" | custom-call | tf_op jit(solution)/shard_map/write/pallas_call | solution.py:603
Async XLA Ops:
  1.3 0.7 %copy-start.4 = (s32[32,1,6]{0,1,2:T(1,128)S(1)}, s32[32,1,6]{0,1,2:T(1,128)}, u32[]{:S(2)}) copy-start(s32[32,1,6]{0,1,2:T(1,128)} %param.10) | copy-start | bytes 2308
  1.3 0.7 %copy-start.5 = (s32[32,1]{0,1:T(1,128)S(1)}, s32[32,1]{0,1:T(1,128)}, u32[]{:S(2)}) copy-start(s32[32,1]{0,1:T(1,128)} %param.9) | copy-start | bytes 388
  1.3 0.7 %copy-start.6 = (s32[32,1]{0,1:T(1,128)S(1)}, s32[32,1]{0,1:T(1,128)}, u32[]{:S(2)}) copy-start(s32[32,1]{0,1:T(1,128)} %param.11) | copy-start | bytes 388
  2.0 1.1 %copy-start = (f32[1,1,5,32,1024]{4,3,2,1,0:T(8,128)S(1)}, f32[1,1,5,32,1024]{4,3,2,1,0:T(8,128)}, u32[]{:S(2)}) copy-start(f32[1,1,5,32,1024]{4,3,2,1,0:T(8,128)} %fine.1) | copy-start | bytes 1966084
  3.1 1.1 %copy-start.1 = (f32[1,1,5,32,1024]{4,3,2,1,0:T(8,128)S(1)}, f32[1,1,5,32,1024]{4,3,2,1,0:T(8,128)}, u32[]{:S(2)}) copy-start(f32[1,1,5,32,1024]{4,3,2,1,0:T(8,128)} %coarse.1) | copy-start | bytes 1966084
  56.8 0.8 %copy-start.2 = (f32[5,32,8,128]{3,2,1,0:T(8,128)}, f32[5,32,8,128]{3,2,1,0:T(8,128)S(1)}, u32[]{:S(2)}) copy-start(f32[5,32,8,128]{3,2,1,0:T(8,128)S(1)} %get-tuple-element.4.fine_result) | copy-start | bytes 1966084
  57.7 0.8 %copy-start.3 = (f32[5,32,8,128]{3,2,1,0:T(8,128)}, f32[5,32,8,128]{3,2,1,0:T(8,128)S(1)}, u32[]{:S(2)}) copy-start(f32[5,32,8,128]{3,2,1,0:T(8,128)S(1)} %get-tuple-element.5.coarse_result) | copy-start | bytes 1966084

commit v4 on v3

v4 whole, which is shorter than its diff:
```python
import jax
import jax.numpy as jnp
from jax import lax
from jax.experimental import pallas as pl
from jax.experimental.pallas import tpu as pltpu
from jax.sharding import PartitionSpec as P

MESH = pl.DeviceIdType.MESH
F32 = jnp.float32
COARSE_STEP = 0.035
TILE = (8, 128)
PATCH = (5, 32, 8, 128)
CHUNK = 4
CHUNKS = 32 // CHUNK
FIRST = 1
COARSE_BREAK = 4


def lanes():
    return lax.broadcasted_iota(jnp.int32, TILE, 1)


def rows():
    return lax.broadcasted_iota(jnp.int32, TILE, 0)


def primitives(cells):
    density, mom_x, mom_y, mom_z, energy = cells
    inverse = 1.0 / density
    vel = [mom_x * inverse, mom_y * inverse, mom_z * inverse]
    kinetic = 0.5 * (mom_x * vel[0] + mom_y * vel[1] + mom_z * vel[2])
    pressure = 0.4 * (energy - kinetic)
    half_sound = 0.5 * jnp.sqrt(1.4 * pressure * inverse)
    return (*vel, pressure, half_sound)


def half_flux(cells, prims, direction):
    half_normal = 0.5 * prims[direction]
    pressure, half_sound = prims[3], prims[4]
    flux = [cells[1 + i] * half_normal for i in range(3)]
    flux[direction] = flux[direction] + 0.5 * pressure
    flux.append((cells[4] + pressure) * half_normal)
    return flux, jnp.abs(half_normal) + half_sound


def interface(low, low_flux, low_speed, high, high_flux, high_speed, direction, sign=None):
    fastest = jnp.maximum(low_speed, high_speed)
    if sign is not None:
        fastest = fastest * sign
    out = [0.5 * (low[1 + direction] + high[1 + direction]) - fastest * (high[0] - low[0])]
    for i in range(4):
        out.append((low_flux[i] + high_flux[i]) - fastest * (high[1 + i] - low[1 + i]))
    return out


def z_up(v):
    return pltpu.roll(v, 127, 1)


def z_down(v):
    return pltpu.roll(v, 1, 1)


def y_up(v):
    return pltpu.roll(jnp.where(lanes() < 32, pltpu.roll(v, 7, 0), v), 96, 1)


def y_down(v):
    return pltpu.roll(jnp.where(lanes() >= 96, pltpu.roll(v, 1, 0), v), 32, 1)


def edge_masks(direction):
    if direction == 1:
        return (rows() == 0) & (lanes() < 32), (rows() == 7) & (lanes() >= 96)
    return lanes() % 32 == 0, lanes() % 32 == 31


def face_sign(direction):
    lower = rows() < 4 if direction == 1 else lanes() % 32 < 16
    return jnp.where(lower, -1.0, 1.0).astype(F32)


def across(cells, prims, direction, outer):
    up, down = (y_up, y_down) if direction == 1 else (z_up, z_down)
    flux, speed = half_flux(cells, prims, direction)
    inner = interface(
        cells, flux, speed, [up(v) for v in cells], [up(v) for v in flux], up(speed), direction
    )
    border = outer(flux, speed)
    lower, upper = edge_masks(direction)
    change = [
        jnp.where(upper, border[i], inner[i]) - jnp.where(lower, border[i], down(inner[i])) for i in range(5)
    ]
    return change, border


def load_plane(ref, x):
    return [ref[f, x] for f in range(5)]


def prepare(state, x):
    cells = load_plane(state, x)
    prims = primitives(cells)
    flux, speed = half_flux(cells, prims, 0)
    return cells, prims, flux, speed


def lowest_interface(state):
    ghost, _, ghost_flux, ghost_speed = prepare(state, 0)
    first, _, flux, speed = prepare(state, 1)
    return interface(ghost, ghost_flux, ghost_speed, first, flux, speed, 0)


def advance(state, first, count, below, update):
    cells, prims, flux, speed = prepare(state, first)
    for n in range(count):
        after = prepare(state, first + n + 1)
        above = interface(cells, flux, speed, after[0], after[2], after[3], 0)
        new = update(first + n - 1, cells, prims, [above[i] - below[i] for i in range(5)])
        for f in range(5):
            state[f, first + n] = new[f]
        cells, prims, flux, speed = after
        below = above
    return below


def pack_y(flat, first, side):
    out = None
    for g in range(4):
        part = flat[pl.ds(first + g * 8 + 7 * side, 8, stride=32), :]
        part = pltpu.roll(part, (32 * g - 96 * side) % 128, 1)
        out = part if g == 0 else jnp.where(lanes() // 32 == g, part, out)
    return out


def pack_z(plane, x, side, out):
    return jnp.where(lanes() % 32 == x, pltpu.roll(plane, (x + 128 - 31 * side) % 128, 1), out)


def pack_z_faces(ref, first):
    def pack(x, carried):
        return tuple(
            pack_z(ref[f, first + x], x, side, carried[side * 5 + f]) for side in range(2) for f in range(5)
        )

    return lax.fori_loop(0, 32, pack, (jnp.zeros(TILE, F32),) * 10, unroll=4)


def spread_y(face, field, x, side):
    row = jnp.broadcast_to(face[field, pl.ds(x // 4, 1), :], TILE)
    shift = (3 - x % 4) * 32 if side else (4 - x % 4) * 32
    return pltpu.roll(row, shift % 128, 1)


def spread_z(face, field, x, side):
    return pltpu.roll(face[field], (128 - x + 31 * side) % 128, 1)


def step_kernel(
    partner, neighbours, work, link, fine, coarse, fine_out, coarse_out,
    held, relay, faces, messages, landed, ghosts,
    state, outer_y, outer_z, register, x_register, packed_z, carry, squeezed,
    coarse_state, flux_y, flux_z, flux_x, note, notes, totals,
    load_sem, coarse_sem, store_sem, coarse_store_sem, ghost_send, ghost_recv, note_send, note_recv,
    near_send, near_recv, far_send, far_recv, up_send, up_recv, on_send, on_recv,
):
    slab = lax.axis_index("slab")
    lvl = lax.axis_index("lvl")
    other_lvl = lvl ^ 2
    own = held.at[0]

    def loads_of(source, target, sem):
        return [
            pltpu.make_async_copy(source.at[0, 0, :, :, pl.ds(j * 128, 128)], target.at[:, :, j, :], sem.at[j])
            for j in range(8)
        ]

    fine_loads = loads_of(fine, own, load_sem)
    coarse_loads = loads_of(coarse, coarse_state.at[:, pl.ds(1, 32)], coarse_sem)
    for copy in fine_loads + coarse_loads:
        copy.start()

    barrier = pltpu.get_barrier_semaphore()
    greeted = [(slab ^ turn, lvl) for turn in range(1, 32)]
    greeted += [(slab, lvl ^ turn) for turn in range(1, 4)] + [(slab ^ 16, other_lvl)]
    for device in greeted:
        pl.semaphore_signal(barrier, inc=1, device_id=device, device_id_type=MESH)

    def span(ref, piece):
        return ref.at[:, pl.ds(piece * CHUNK, CHUNK)]

    def near(axis, piece):
        return pltpu.make_async_remote_copy(
            src_ref=span(own, piece), dst_ref=span(held.at[1 + 2 * axis], piece),
            send_sem=near_send.at[axis, piece], recv_sem=near_recv.at[axis, piece],
            device_id=(slab ^ (4 if axis else 1), lvl), device_id_type=MESH,
        )

    def far(axis, piece):
        return pltpu.make_async_remote_copy(
            src_ref=span(held.at[1 + 2 * axis], piece), dst_ref=span(held.at[2 + 2 * axis], piece),
            send_sem=far_send.at[axis, piece], recv_sem=far_recv.at[axis, piece],
            device_id=(slab ^ (12 if axis else 3), lvl), device_id_type=MESH,
        )

    def up(piece):
        return pltpu.make_async_remote_copy(
            src_ref=span(own, piece), dst_ref=span(relay, piece),
            send_sem=up_send.at[piece], recv_sem=up_recv.at[piece],
            device_id=(slab ^ (piece % 2 * 16), other_lvl), device_id_type=MESH,
        )

    def on(piece):
        return pltpu.make_async_remote_copy(
            src_ref=span(relay, piece), dst_ref=span(held.at[5], piece),
            send_sem=on_send.at[piece], recv_sem=on_recv.at[piece],
            device_id=(slab ^ ((piece + 1) % 2 * 16), other_lvl), device_id_type=MESH,
        )

    def send(piece):
        near(0, piece).start()
        near(1, piece).start()
        up(piece).start()

    def forward(piece):
        for axis in range(2):
            near(axis, piece).wait_recv()
            far(axis, piece).start()
        up(piece).wait_recv()
        on(piece).start()

    def arrive(piece):
        far(0, piece).wait_recv()
        far(1, piece).wait_recv()
        on(piece).wait_recv()

    for copy in fine_loads:
        copy.wait()
    pl.semaphore_wait(barrier, len(greeted))
    for piece in range(FIRST):
        send(piece)

    flat = own.reshape(5 * 32 * 8, 128)
    for f in range(5):
        faces[0, f] = own[f, 0]
        faces[1, f] = own[f, 31]
        for side in range(2):
            faces[2 + side, f] = pack_y(flat, f * 256, side)
    packed = pack_z_faces(own, 0)
    for side in range(2):
        for f in range(5):
            faces[4 + side, f] = packed[side * 5 + f]

    mine = [neighbours[f, 0, slab] for f in range(6)]
    ghost_copies = []
    for turn in range(32):
        there = slab ^ turn
        patch = partner[0, there]
        which = jnp.int32(0)
        for f in range(1, 6):
            which = jnp.where(mine[f] == patch, f, which)
        target = messages if turn else landed
        for f in range(5):
            target[turn, f] = faces[which, f]
        if turn:
            copy = pltpu.make_async_remote_copy(
                src_ref=messages.at[turn], dst_ref=landed.at[turn],
                send_sem=ghost_send.at[turn], recv_sem=ghost_recv.at[turn],
                device_id=(there, lvl), device_id_type=MESH,
            )
            copy.start()
            ghost_copies.append(copy)
    for piece in range(FIRST, CHUNKS):
        send(piece)

    for copy in coarse_loads:
        copy.wait()
    for f in range(5):
        coarse_state[f, 0] = coarse_state[f, 1]
        coarse_state[f, 33] = coarse_state[f, 32]

    def coarse_update(x, cells, prims, change):
        for d, kept in ((1, flux_y), (2, flux_z)):

            def border(flux, speed, d=d):
                return [cells[1 + d]] + [2.0 * v for v in flux]

            part, values = across(cells, prims, d, border)
            change = [change[i] + part[i] for i in range(5)]
            for i in range(5):
                kept[i, x] = values[i]
        return [cells[i] - COARSE_STEP * change[i] for i in range(5)]

    lowest = lowest_interface(coarse_state)

    def coarse_chunk(c, below):
        return tuple(advance(coarse_state, 1 + c * CHUNK, CHUNK, below, coarse_update))

    highest = lax.fori_loop(0, COARSE_BREAK, coarse_chunk, tuple(lowest))
    forward(0)
    highest = lax.fori_loop(COARSE_BREAK, CHUNKS, coarse_chunk, highest)
    for i in range(5):
        flux_x[0, i] = lowest[i]
        flux_x[1, i] = highest[i]

    code = link[0, 0]
    valid = code >= 0
    level = jnp.maximum(code, 0) // 24
    face = jnp.maximum(code, 0) % 24 // 4
    quarter = jnp.maximum(code, 0) % 4
    direction, side = face // 2, face % 2
    quarter_row = jnp.where(direction == 2, quarter % 2, quarter // 2)
    quarter_col = jnp.where(direction == 2, quarter // 2, quarter % 2)

    source = partner[0, slab]
    apart = source ^ slab
    chosen = jnp.int32(0)
    for bit in range(5):
        chosen = chosen + (apart >= (1 << bit)).astype(jnp.int32)
    linked = [neighbours[f, 0, source] for f in range(6)]
    present = [linked[f] >= 0 for f in range(6)]
    count = work[0, source]
    steps = jnp.full(TILE, count.astype(F32), F32)
    ratio = 2.0 * COARSE_STEP / steps
    share = 1.0 / steps

    def choose(piece):
        for n in range(CHUNK):
            x = piece * CHUNK + n
            for f in range(5):
                value = held[0, f, x]
                for k in range(1, 6):
                    value = jnp.where(chosen == k, held[k, f, x], value)
                state[f, x + 1] = value

    def spread(x):
        cells = load_plane(state, x + 1)
        for d, spreader, outer in ((1, spread_y, outer_y), (2, spread_z, outer_z)):
            lower = rows() < 4 if d == 1 else lanes() % 32 < 16
            values = []
            for f in range(5):
                low = jnp.where(present[2 * d], spreader(ghosts.at[2 * d], f, x, 0), cells[f])
                high = jnp.where(present[2 * d + 1], spreader(ghosts.at[2 * d + 1], f, x, 1), cells[f])
                values.append(jnp.where(lower, low, high))
            flux, speed = half_flux(values, primitives(values), d)
            for i, v in enumerate(values + flux + [speed]):
                outer[i, x] = v

    def updater(substep):
        active = substep < count

        def update(x, cells, prims, change):
            borders = []
            for d, outer in ((1, outer_y), (2, outer_z)):

                def border(flux, speed, d=d, outer=outer):
                    return interface(
                        cells, flux, speed, [outer[i, x] for i in range(5)],
                        [outer[5 + i, x] for i in range(4)], outer[9, x], d, face_sign(d),
                    )

                part, values = across(cells, prims, d, border)
                borders.append(values)
                change = [change[i] + part[i] for i in range(5)]
            for i in range(5):
                value = jnp.where(direction == 1, borders[0][i], borders[1][i])
                value = jnp.where(active, value * share, 0.0)
                register[i, x] = value if substep == 0 else register[i, x] + value
            return [jnp.where(active, cells[i] - ratio * change[i], cells[i]) for i in range(5)]

        return update

    def outermost(substep, wanted, values):
        for i in range(5):
            value = jnp.where((substep < count) & (side == wanted), values[i] * share, 0.0)
            x_register[i] = value if substep == 0 and wanted == 0 else x_register[i] + value

    def pack_register(first, planes):
        for f in range(5):
            value = packed_z[f]
            for n in range(planes):
                value = pack_z(register[f, first + n], first + n, side, value)
            packed_z[f] = value

    def stores_of(piece):
        first = pl.multiple_of(piece * 8, 8)
        return [
            pltpu.make_async_copy(
                state.at[:, pl.ds(first + 1, 8), j, :],
                fine_out.at[0, 0, :, pl.ds(first, 8), pl.ds(j * 128, 128)],
                store_sem.at[piece, j],
            )
            for j in range(8)
        ]

    forward(1)
    for copy in ghost_copies:
        copy.wait_recv()
    for f in range(6):
        turn = jnp.maximum(linked[f], 0) ^ slab
        for i in range(5):
            ghosts[f, i] = landed[turn, i]
    arrive(0)
    choose(0)
    for f in range(5):
        state[f, 0] = jnp.where(present[0], ghosts[0, f], state[f, 1])
        packed_z[f] = jnp.zeros(TILE, F32)
    for x in range(CHUNK - 1):
        spread(x)
    for substep in range(4):
        lowest = lowest_interface(state)
        outermost(substep, 0, lowest)
        reach = CHUNK - 1 - substep
        below = advance(state, 1, reach, lowest, updater(substep)) if reach > 0 else lowest
        for i in range(5):
            carry[substep, i] = below[i]

    def wave(c, _):
        @pl.when(c < CHUNKS - 1)
        def _():
            forward(c + 1)

        arrive(c)
        choose(c)
        for n in range(CHUNK):
            spread(c * CHUNK - 1 + n)
        for substep in range(4):
            below = [carry[substep, i] for i in range(5)]
            below = advance(state, c * CHUNK - substep, CHUNK, below, updater(substep))
            for i in range(5):
                carry[substep, i] = below[i]
        pack_register((c - 1) * CHUNK, CHUNK)

        @pl.when(c % 2 == 0)
        def _():
            for copy in stores_of(c // 2 - 1):
                copy.start()

        return 0

    lax.fori_loop(1, CHUNKS, wave, 0)
    for f in range(5):
        state[f, 33] = jnp.where(present[1], ghosts[1, f], state[f, 32])
    spread(31)
    for substep in range(4):
        below = [carry[substep, i] for i in range(5)]
        outermost(substep, 1, advance(state, 32 - substep, substep + 1, below, updater(substep)))
    pack_register(32 - CHUNK, CHUNK)

    flat = register.reshape(5 * 32 * 8, 128)
    source_lane = lax.broadcasted_iota(jnp.int32, (128, 128), 0)
    target_lane = lax.broadcasted_iota(jnp.int32, (128, 128), 1)
    wanted = target_lane // 32 * 64 + target_lane % 32 * 2
    squeeze = ((source_lane == wanted) & (target_lane % 32 < 16) & (target_lane < 64)).astype(F32)
    for f in range(5):
        value = jnp.where(direction == 1, pack_y(flat, f * 256, side), packed_z[f])
        value = jnp.where(direction == 0, x_register[f], value)
        value = value + pltpu.roll(value, 127, 1)
        squeezed[pl.ds(f * 8, 8), :] = 0.25 * (value + pltpu.roll(value, 96, 1))
    squeezed[...] = jnp.dot(
        squeezed[...], squeeze, precision=lax.Precision.HIGHEST, preferred_element_type=F32
    )
    low_lanes = lax.broadcasted_iota(jnp.int32, (4, 128), 1) < 64
    for f in range(5):
        even = squeezed[pl.ds(f * 8, 4, stride=2), :]
        odd = squeezed[pl.ds(f * 8 + 1, 4, stride=2), :]
        small = jnp.where(low_lanes, even, pltpu.roll(odd, 64, 1))
        small = jnp.where(quarter_col == 0, small, pltpu.roll(small, 16, 1))
        note[f, pl.ds(0, 4), :] = jnp.where(quarter_row == 0, small, 0.0)
        note[f, pl.ds(4, 4), :] = jnp.where(quarter_row == 1, small, 0.0)
    place = level * 6 + (face ^ 1) + 1
    inside = (rows() // 4 == quarter_row) & (lanes() % 32 // 16 == quarter_col)
    note[5] = jnp.where(inside & valid, place.astype(F32), 0.0)
    note_copies = []
    for turn in range(1, 4):
        copy = pltpu.make_async_remote_copy(
            src_ref=note, dst_ref=notes.at[turn - 1],
            send_sem=note_send.at[turn - 1], recv_sem=note_recv.at[turn - 1],
            device_id=(slab, lvl ^ turn), device_id_type=MESH,
        )
        copy.start()
        note_copies.append(copy)
    for copy in stores_of(3):
        copy.start()

    for copy in ghost_copies:
        copy.wait_send()
    for piece in range(CHUNKS):
        for axis in range(2):
            near(axis, piece).wait_send()
            far(axis, piece).wait_send()
        up(piece).wait_send()
        on(piece).wait_send()

    for copy in note_copies:
        copy.wait_recv()
    for g in range(6):
        key = (lvl * 6 + g + 1).astype(F32)
        parts = [note if n == 3 else notes.at[n] for n in range(4)]
        hits = [part[5] == key for part in parts]
        for f in range(5):
            total = jnp.zeros(TILE, F32)
            for n in range(4):
                total = total + jnp.where(hits[n], parts[n][f], 0.0)
            totals[g, f] = total
        cover = jnp.zeros(TILE, F32)
        for n in range(4):
            cover = cover + jnp.where(hits[n], 1.0, 0.0)
        totals[g, 5] = cover

    for end, x in ((0, 1), (1, 32)):
        for f in range(5):
            amount = totals[end, 5] * flux_x[end, f] - totals[end, f]
            coarse_state[f, x] = coarse_state[f, x] + (COARSE_STEP if end else -COARSE_STEP) * amount

    def correct(x):
        cells = load_plane(coarse_state, x + 1)
        for d, spreader, kept in ((1, spread_y, flux_y), (2, spread_z, flux_z)):
            lower, upper = edge_masks(d)
            weight = COARSE_STEP * face_sign(d) * (lower | upper).astype(F32)

            def both(f, d=d, spreader=spreader, upper=upper):
                low = spreader(totals.at[2 * d], f, x, 0)
                high = spreader(totals.at[2 * d + 1], f, x, 1)
                return jnp.where(upper, high, low)

            cover = both(5)
            for f in range(5):
                cells[f] = cells[f] + weight * (cover * kept[f, x] - both(f))
        for f in range(5):
            coarse_state[f, x + 1] = cells[f]

    def coarse_stores_of(piece):
        first = pl.multiple_of(piece * 8, 8)
        return [
            pltpu.make_async_copy(
                coarse_state.at[:, pl.ds(first + 1, 8), j, :],
                coarse_out.at[0, 0, :, pl.ds(first, 8), pl.ds(j * 128, 128)],
                coarse_store_sem.at[piece, j],
            )
            for j in range(8)
        ]

    def correct_eight(piece, _):
        for n in range(8):
            correct(piece * 8 + n)
        for copy in coarse_stores_of(piece):
            copy.start()
        return 0

    lax.fori_loop(0, 4, correct_eight, 0)
    for copy in note_copies:
        copy.wait_send()
    for piece in range(4):
        for copy in stores_of(piece) + coarse_stores_of(piece):
            copy.wait()


def write_kernel(fine_result, coarse_result, fine_out, coarse_out, sem):
    copies = [
        pltpu.make_async_copy(source.at[0, 0, f], target.at[0, 0, f], sem.at[n, f])
        for n, (source, target) in enumerate(((fine_result, fine_out), (coarse_result, coarse_out)))
        for f in range(5)
    ]
    for copy in copies:
        copy.start()
    for copy in copies:
        copy.wait()


SMEM = pl.BlockSpec(memory_space=pltpu.SMEM)
HBM = pl.BlockSpec(memory_space=pltpu.HBM)
DMA = pltpu.SemaphoreType.DMA
LIMIT = 60 * 1024 * 1024


def step(partner, neighbours, work, link, fine_state, coarse_state):
    return pl.pallas_call(
        step_kernel,
        out_shape=(jax.ShapeDtypeStruct(fine_state.shape, F32), jax.ShapeDtypeStruct(coarse_state.shape, F32)),
        in_specs=[SMEM, SMEM, SMEM, SMEM, HBM, HBM],
        out_specs=(HBM, HBM),
        scratch_shapes=[
            pltpu.VMEM((6, *PATCH), F32),
            pltpu.VMEM(PATCH, F32),
            pltpu.VMEM((6, 5, *TILE), F32),
            pltpu.VMEM((32, 5, *TILE), F32),
            pltpu.VMEM((32, 5, *TILE), F32),
            pltpu.VMEM((6, 5, *TILE), F32),
            pltpu.VMEM((5, 34, *TILE), F32),
            pltpu.VMEM((10, 32, *TILE), F32),
            pltpu.VMEM((10, 32, *TILE), F32),
            pltpu.VMEM(PATCH, F32),
            pltpu.VMEM((5, *TILE), F32),
            pltpu.VMEM((5, *TILE), F32),
            pltpu.VMEM((4, 5, *TILE), F32),
            pltpu.VMEM((40, 128), F32),
            pltpu.VMEM((5, 34, *TILE), F32),
            pltpu.VMEM(PATCH, F32),
            pltpu.VMEM(PATCH, F32),
            pltpu.VMEM((2, 5, *TILE), F32),
            pltpu.VMEM((6, *TILE), F32),
            pltpu.VMEM((3, 6, *TILE), F32),
            pltpu.VMEM((6, 6, *TILE), F32),
            DMA((8,)), DMA((8,)), DMA((4, 8)), DMA((4, 8)), DMA((32,)), DMA((32,)), DMA((3,)), DMA((3,)),
            DMA((2, CHUNKS)), DMA((2, CHUNKS)), DMA((2, CHUNKS)), DMA((2, CHUNKS)),
            DMA((CHUNKS,)), DMA((CHUNKS,)), DMA((CHUNKS,)), DMA((CHUNKS,)),
        ],
        compiler_params=pltpu.CompilerParams(collective_id=0, has_side_effects=True, vmem_limit_bytes=LIMIT),
        name="step",
    )(partner, neighbours, work, link, fine_state, coarse_state)


def write(fine_result, coarse_result):
    return pl.pallas_call(
        write_kernel,
        out_shape=tuple(jax.ShapeDtypeStruct(v.shape, F32) for v in (fine_result, coarse_result)),
        in_specs=[HBM, HBM],
        out_specs=(HBM, HBM),
        scratch_shapes=[DMA((2, 5))],
        compiler_params=pltpu.CompilerParams(vmem_limit_bytes=LIMIT),
        name="write",
    )(fine_result, coarse_result)


def body(fine_state, coarse_state, partner, mig_slot, neighbours, work, coarse_link):
    del mig_slot
    results = step(
        partner.T, jnp.transpose(neighbours, (2, 1, 0)), work.T, coarse_link, fine_state, coarse_state
    )
    return write(*results)


def solution(mesh):
    return jax.shard_map(
        body,
        mesh=mesh,
        in_specs=(
            P("slab", "lvl", None, None, None),
            P("slab", "lvl", None, None, None),
            P(None, "lvl"),
            P(None, "lvl"),
            P(None, "lvl", None),
            P(None, "lvl"),
            P("slab", "lvl"),
        ),
        out_specs=(P("slab", "lvl", None, None, None), P("slab", "lvl", None, None, None)),
        check_vma=False,
    )
```

time: 61.2 us -> 101 us (1.65)
  Pallas kernels: 55.1 us -> 99 us
  local copies, waits for them, and re-layouts: 4.51 us -> 0 us
    pallas_call x2, Pallas kernels: 55.1 us -> 99 us  [the longest x1 58.1 us: step(): pl.pallas_call(step_kernel, out_shape=(jax.ShapeDtypeStruct(fine_state.sh...]
    unnamed x14 -> x0, local copies, waits for them, and re-layouts: 4.51 us -> none
where the time goes in v4:
time: 101 us; the launch traced here: 100 us
  Pallas kernels  99 us (98%)
  between operations  1.29 us (1%)
    pallas_call x1, Pallas kernels, step(): pl.pallas_call(step_kernel, out_shape=(jax.ShapeDtypeStruct(fine_state.sh...  58.1 us
    pallas_call x1, Pallas kernels, write(): pl.pallas_call(write_kernel, out_shape=tuple((jax.ShapeDtypeStruct(v.shap...  40.9 us

profile of v4, /device:TPU:1, one launch (start us, length us, event | category | flops | bytes accessed | tf_op | source)
XLA Modules:
  0.0 100.3 jit_solution(18048898865761319805)
XLA Ops:
  1.3 58.1 %step.1 = (f32[1,1,5,32,1024]{4,3,2,1,0:T(8,128)}, f32[1,1,5,32,1024]{4,3,2,1,0:T(8,128)}) custom-call(s32[1,32]{1,0:T(1,128)} %bitcast.4, s32[6,1,32]{2,1,0:T(1,128)} %bitcast.3, s32[1,32]{1,0:T(1,128)} %bitcast.5, s32[1,1]{1,0:T(1,128)S(6)} %copy.8.link, f32[1,1,5,32,1024]{4,3,2,1,0:T(8,128)} %fine.1, f32[1,1,5,32,1024]{4,3,2,1,0:T(8,128)} %coarse.1), custom_call_target="tpu_custom_call" | custom-call | tf_op jit(solution)/shard_map/step/pallas_call | solution.py:578
  59.4 40.9 %write.1 = (f32[1,1,5,32,1024]{4,3,2,1,0:T(8,128)}, f32[1,1,5,32,1024]{4,3,2,1,0:T(8,128)}) custom-call(f32[1,1,5,32,1024]{4,3,2,1,0:T(8,128)} %get-tuple-element.4.fine_result, f32[1,1,5,32,1024]{4,3,2,1,0:T(8,128)} %get-tuple-element.5.coarse_result), custom_call_target="tpu_custom_call" | custom-call | tf_op jit(solution)/shard_map/write/pallas_call | solution.py:615

commit v5 on v4

--- a/solution.py
+++ b/solution.py
@@ -12,8 +12,12 @@
 PATCH = (5, 32, 8, 128)
 CHUNK = 4
 CHUNKS = 32 // CHUNK
-FIRST = 1
-COARSE_BREAK = 4
+PIECE = 2
+PIECES = 32 // PIECE
+FIRST = 2
+QUEUE = 4
+BESIDE = 4
+AHEAD = 4
 
 
 def lanes():
@@ -94,6 +98,14 @@
     return change, border
 
 
+def each(first, last, act):
+    def one(i, _):
+        act(i)
+        return 0
+
+    lax.fori_loop(first, last, one, 0)
+
+
 def load_plane(ref, x):
     return [ref[f, x] for f in range(5)]
 
@@ -157,10 +169,10 @@
 
 
 def step_kernel(
-    partner, neighbours, work, link, fine, coarse, fine_out, coarse_out,
+    partner, neighbours, work, link, fine, coarse, fine_out, coarse_out, amounts,
     held, relay, faces, messages, landed, ghosts,
     state, outer_y, outer_z, register, x_register, packed_z, carry, squeezed,
-    coarse_state, flux_y, flux_z, flux_x, note, notes, totals,
+    coarse_state, flux_y, flux_z, flux_faces, note, notes,
     load_sem, coarse_sem, store_sem, coarse_store_sem, ghost_send, ghost_recv, note_send, note_recv,
     near_send, near_recv, far_send, far_recv, up_send, up_recv, on_send, on_recv,
 ):
@@ -181,13 +193,16 @@
         copy.start()
 
     barrier = pltpu.get_barrier_semaphore()
-    greeted = [(slab ^ turn, lvl) for turn in range(1, 32)]
-    greeted += [(slab, lvl ^ turn) for turn in range(1, 4)] + [(slab ^ 16, other_lvl)]
-    for device in greeted:
+
+    def greet(device):
         pl.semaphore_signal(barrier, inc=1, device_id=device, device_id_type=MESH)
 
+    each(1, 32, lambda turn: greet((slab ^ turn, lvl)))
+    each(1, 4, lambda turn: greet((slab, lvl ^ turn)))
+    greet((slab ^ 16, other_lvl))
+
     def span(ref, piece):
-        return ref.at[:, pl.ds(piece * CHUNK, CHUNK)]
+        return ref.at[:, pl.ds(piece * PIECE, PIECE)]
 
     def near(axis, piece):
         return pltpu.make_async_remote_copy(
@@ -229,6 +244,13 @@
         up(piece).wait_recv()
         on(piece).start()
 
+    def relay_on(piece):
+        forward(piece)
+
+        @pl.when(piece + QUEUE < PIECES)
+        def _():
+            send(piece + QUEUE)
+
     def arrive(piece):
         far(0, piece).wait_recv()
         far(1, piece).wait_recv()
@@ -236,9 +258,8 @@
 
     for copy in fine_loads:
         copy.wait()
-    pl.semaphore_wait(barrier, len(greeted))
-    for piece in range(FIRST):
-        send(piece)
+    pl.semaphore_wait(barrier, 35)
+    each(0, FIRST, send)
 
     flat = own.reshape(5 * 32 * 8, 128)
     for f in range(5):
@@ -252,26 +273,29 @@
             faces[4 + side, f] = packed[side * 5 + f]
 
     mine = [neighbours[f, 0, slab] for f in range(6)]
-    ghost_copies = []
-    for turn in range(32):
-        there = slab ^ turn
-        patch = partner[0, there]
+
+    def compose(turn, target):
+        patch = partner[0, slab ^ turn]
         which = jnp.int32(0)
         for f in range(1, 6):
             which = jnp.where(mine[f] == patch, f, which)
-        target = messages if turn else landed
         for f in range(5):
             target[turn, f] = faces[which, f]
-        if turn:
-            copy = pltpu.make_async_remote_copy(
-                src_ref=messages.at[turn], dst_ref=landed.at[turn],
-                send_sem=ghost_send.at[turn], recv_sem=ghost_recv.at[turn],
-                device_id=(there, lvl), device_id_type=MESH,
-            )
-            copy.start()
-            ghost_copies.append(copy)
-    for piece in range(FIRST, CHUNKS):
-        send(piece)
+
+    def ghost(turn):
+        return pltpu.make_async_remote_copy(
+            src_ref=messages.at[turn], dst_ref=landed.at[turn],
+            send_sem=ghost_send.at[turn], recv_sem=ghost_recv.at[turn],
+            device_id=(slab ^ turn, lvl), device_id_type=MESH,
+        )
+
+    def send_ghost(turn):
+        compose(turn, messages)
+        ghost(turn).start()
+
+    compose(0, landed)
+    each(1, 32, send_ghost)
+    each(FIRST, QUEUE, send)
 
     for copy in coarse_loads:
         copy.wait()
@@ -296,12 +320,24 @@
     def coarse_chunk(c, below):
         return tuple(advance(coarse_state, 1 + c * CHUNK, CHUNK, below, coarse_update))
 
-    highest = lax.fori_loop(0, COARSE_BREAK, coarse_chunk, tuple(lowest))
-    forward(0)
-    highest = lax.fori_loop(COARSE_BREAK, CHUNKS, coarse_chunk, highest)
-    for i in range(5):
-        flux_x[0, i] = lowest[i]
-        flux_x[1, i] = highest[i]
+
+    def coarse_part(n, below):
+        below = lax.fori_loop(n * CHUNKS // BESIDE, (n + 1) * CHUNKS // BESIDE, coarse_chunk, below)
+        relay_on(n)
+        return below
+
+    highest = lax.fori_loop(0, BESIDE, coarse_part, tuple(lowest))
+    coarse_store = pltpu.make_async_copy(coarse_state.at[:, pl.ds(1, 32)], coarse_out, coarse_store_sem)
+    coarse_store.start()
+    for f in range(5):
+        flux_faces[0, f] = lowest[f]
+        flux_faces[1, f] = highest[f]
+        for end in range(2):
+            flux_faces[2 + end, f] = pack_y(flux_y.reshape(5 * 32 * 8, 128), f * 256, end)
+    packed = pack_z_faces(flux_z, 0)
+    for end in range(2):
+        for f in range(5):
+            flux_faces[4 + end, f] = packed[end * 5 + f]
 
     code = link[0, 0]
     valid = code >= 0
@@ -324,14 +360,13 @@
     ratio = 2.0 * COARSE_STEP / steps
     share = 1.0 / steps
 
-    def choose(piece):
-        for n in range(CHUNK):
-            x = piece * CHUNK + n
+    def choose(first, planes):
+        for n in range(planes):
             for f in range(5):
-                value = held[0, f, x]
+                value = held[0, f, first + n]
                 for k in range(1, 6):
-                    value = jnp.where(chosen == k, held[k, f, x], value)
-                state[f, x + 1] = value
+                    value = jnp.where(chosen == k, held[k, f, first + n], value)
+                state[f, first + n + 1] = value
 
     def spread(x):
         cells = load_plane(state, x + 1)
@@ -393,15 +428,15 @@
             for j in range(8)
         ]
 
-    forward(1)
-    for copy in ghost_copies:
-        copy.wait_recv()
+    each(BESIDE, CHUNK // PIECE + AHEAD, relay_on)
+    each(1, 32, lambda turn: ghost(turn).wait_recv())
     for f in range(6):
         turn = jnp.maximum(linked[f], 0) ^ slab
         for i in range(5):
             ghosts[f, i] = landed[turn, i]
-    arrive(0)
-    choose(0)
+    for piece in range(CHUNK // PIECE):
+        arrive(piece)
+    choose(0, CHUNK)
     for f in range(5):
         state[f, 0] = jnp.where(present[0], ghosts[0, f], state[f, 1])
         packed_z[f] = jnp.zeros(TILE, F32)
@@ -415,20 +450,27 @@
         for i in range(5):
             carry[substep, i] = below[i]
 
-    def wave(c, _):
-        @pl.when(c < CHUNKS - 1)
-        def _():
-            forward(c + 1)
-
-        arrive(c)
-        choose(c)
-        for n in range(CHUNK):
-            spread(c * CHUNK - 1 + n)
+    def follow(first, planes):
+        for n in range(planes // PIECE):
+            arrive(first // PIECE + n)
+        choose(first, planes)
+        for n in range(planes):
+            spread(first - 1 + n)
         for substep in range(4):
             below = [carry[substep, i] for i in range(5)]
-            below = advance(state, c * CHUNK - substep, CHUNK, below, updater(substep))
+            below = advance(state, first - substep, planes, below, updater(substep))
             for i in range(5):
                 carry[substep, i] = below[i]
+
+    def wave(c, _):
+        for n in range(CHUNK // PIECE):
+            piece = c * (CHUNK // PIECE) + AHEAD + n
+
+            @pl.when(piece < PIECES)
+            def _(piece=piece):
+                relay_on(piece)
+
+        follow(c * CHUNK, CHUNK)
         pack_register((c - 1) * CHUNK, CHUNK)
 
         @pl.when(c % 2 == 0)
@@ -438,7 +480,9 @@
 
         return 0
 
-    lax.fori_loop(1, CHUNKS, wave, 0)
+    lax.fori_loop(1, CHUNKS - 1, wave, 0)
+    each(0, CHUNK // PIECE, lambda n: follow(32 - CHUNK + n * PIECE, PIECE))
+    pack_register(32 - 2 * CHUNK, CHUNK)
     for f in range(5):
         state[f, 33] = jnp.where(present[1], ghosts[1, f], state[f, 32])
     spread(31)
@@ -483,14 +527,16 @@
     for copy in stores_of(3):
         copy.start()
 
-    for copy in ghost_copies:
-        copy.wait_send()
-    for piece in range(CHUNKS):
+    each(1, 32, lambda turn: ghost(turn).wait_send())
+
+    def sent(piece):
         for axis in range(2):
             near(axis, piece).wait_send()
             far(axis, piece).wait_send()
         up(piece).wait_send()
         on(piece).wait_send()
+
+    each(0, PIECES, sent)
 
     for copy in note_copies:
         copy.wait_recv()
@@ -498,77 +544,92 @@
         key = (lvl * 6 + g + 1).astype(F32)
         parts = [note if n == 3 else notes.at[n] for n in range(4)]
         hits = [part[5] == key for part in parts]
+        cover = jnp.zeros(TILE, F32)
+        for n in range(4):
+            cover = cover + jnp.where(hits[n], 1.0, 0.0)
         for f in range(5):
             total = jnp.zeros(TILE, F32)
             for n in range(4):
                 total = total + jnp.where(hits[n], parts[n][f], 0.0)
-            totals[g, f] = total
-        cover = jnp.zeros(TILE, F32)
-        for n in range(4):
-            cover = cover + jnp.where(hits[n], 1.0, 0.0)
-        totals[g, 5] = cover
-
-    for end, x in ((0, 1), (1, 32)):
-        for f in range(5):
-            amount = totals[end, 5] * flux_x[end, f] - totals[end, f]
-            coarse_state[f, x] = coarse_state[f, x] + (COARSE_STEP if end else -COARSE_STEP) * amount
-
-    def correct(x):
-        cells = load_plane(coarse_state, x + 1)
-        for d, spreader, kept in ((1, spread_y, flux_y), (2, spread_z, flux_z)):
-            lower, upper = edge_masks(d)
-            weight = COARSE_STEP * face_sign(d) * (lower | upper).astype(F32)
-
-            def both(f, d=d, spreader=spreader, upper=upper):
-                low = spreader(totals.at[2 * d], f, x, 0)
-                high = spreader(totals.at[2 * d + 1], f, x, 1)
-                return jnp.where(upper, high, low)
-
-            cover = both(5)
-            for f in range(5):
-                cells[f] = cells[f] + weight * (cover * kept[f, x] - both(f))
-        for f in range(5):
-            coarse_state[f, x + 1] = cells[f]
-
-    def coarse_stores_of(piece):
-        first = pl.multiple_of(piece * 8, 8)
-        return [
-            pltpu.make_async_copy(
-                coarse_state.at[:, pl.ds(first + 1, 8), j, :],
-                coarse_out.at[0, 0, :, pl.ds(first, 8), pl.ds(j * 128, 128)],
-                coarse_store_sem.at[piece, j],
-            )
-            for j in range(8)
-        ]
-
-    def correct_eight(piece, _):
-        for n in range(8):
-            correct(piece * 8 + n)
-        for copy in coarse_stores_of(piece):
-            copy.start()
-        return 0
-
-    lax.fori_loop(0, 4, correct_eight, 0)
+            amounts[g, f] = (COARSE_STEP if g % 2 else -COARSE_STEP) * (cover * flux_faces[g, f] - total)
     for copy in note_copies:
         copy.wait_send()
-    for piece in range(4):
-        for copy in stores_of(piece) + coarse_stores_of(piece):
+    coarse_store.wait()
+
+    def stored(piece):
+        for copy in stores_of(piece):
             copy.wait()
 
-
-def write_kernel(fine_result, coarse_result, fine_out, coarse_out, sem):
-    copies = [
-        pltpu.make_async_copy(source.at[0, 0, f], target.at[0, 0, f], sem.at[n, f])
-        for n, (source, target) in enumerate(((fine_result, fine_out), (coarse_result, coarse_out)))
-        for f in range(5)
-    ]
-    for copy in copies:
-        copy.start()
-    for copy in copies:
-        copy.wait()
+    each(0, 4, stored)
+
+
+def finish_kernel(fine, coarse, amounts, fine_out, coarse_out, fine_held, state, fine_sem, coarse_sem, out_sem):
+    def load(n):
+        planes = pl.ds(n * 8, 8)
+        return pltpu.make_async_copy(coarse.at[:, planes], state.at[:, planes], coarse_sem.at[n])
+
+    def store(n, j):
+        first = pl.multiple_of(n * 8, 8)
+        return pltpu.make_async_copy(
+            state.at[:, pl.ds(first, 8), j, :],
+            coarse_out.at[0, 0, :, pl.ds(first, 8), pl.ds(j * 128, 128)],
+            out_sem.at[n, j],
+        )
+
+    def fine_load(f):
+        return pltpu.make_async_copy(fine.at[0, 0, f], fine_held.at[f], fine_sem.at[f])
+
+    def fine_store(f):
+        return pltpu.make_async_copy(fine_held.at[f], fine_out.at[0, 0, f], fine_sem.at[5 + f])
+
+    each(0, 4, lambda n: load(n).start())
+    each(0, 5, lambda f: fine_load(f).start())
+
+    def correct(x):
+        cells = load_plane(state, x)
+        for d, spreader in ((1, spread_y), (2, spread_z)):
+            lower, upper = edge_masks(d)
+            for f in range(5):
+                low = jnp.where(lower, spreader(amounts.at[2 * d], f, x, 0), 0.0)
+                cells[f] = cells[f] + jnp.where(upper, spreader(amounts.at[2 * d + 1], f, x, 1), low)
+        for f in range(5):
+            state[f, x] = cells[f]
+
+    def correct_eight(n):
+        load(n).wait()
+        for end in range(2):
+
+            @pl.when(n == end * 3)
+            def _(end=end):
+                for f in range(5):
+                    state[f, 31 * end] = state[f, 31 * end] + amounts[end, f]
+
+        def correct_four(half):
+            for k in range(4):
+                correct(n * 8 + half * 4 + k)
+
+        each(0, 2, correct_four)
+        for j in range(8):
+            store(n, j).start()
+
+    def pass_on(f):
+        fine_load(f).wait()
+        fine_store(f).start()
+
+    correct_eight(0)
+    each(0, 5, pass_on)
+    each(1, 4, correct_eight)
+    each(0, 5, lambda f: fine_store(f).wait())
+
+    def stored(n):
+        for j in range(8):
+            store(n, j).wait()
+
+    each(0, 4, stored)
 
 
 SMEM = pl.BlockSpec(memory_space=pltpu.SMEM)
+VMEM = pl.BlockSpec(memory_space=pltpu.VMEM)
 HBM = pl.BlockSpec(memory_space=pltpu.HBM)
 DMA = pltpu.SemaphoreType.DMA
 LIMIT = 60 * 1024 * 1024
@@ -577,9 +638,13 @@
 def step(partner, neighbours, work, link, fine_state, coarse_state):
     return pl.pallas_call(
         step_kernel,
-        out_shape=(jax.ShapeDtypeStruct(fine_state.shape, F32), jax.ShapeDtypeStruct(coarse_state.shape, F32)),
+        out_shape=(
+            jax.ShapeDtypeStruct(fine_state.shape, F32),
+            jax.ShapeDtypeStruct(PATCH, F32),
+            jax.ShapeDtypeStruct((6, 5, *TILE), F32),
+        ),
         in_specs=[SMEM, SMEM, SMEM, SMEM, HBM, HBM],
-        out_specs=(HBM, HBM),
+        out_specs=(HBM, HBM, VMEM),
         scratch_shapes=[
             pltpu.VMEM((6, *PATCH), F32),
             pltpu.VMEM(PATCH, F32),
@@ -598,29 +663,31 @@
             pltpu.VMEM((5, 34, *TILE), F32),
             pltpu.VMEM(PATCH, F32),
             pltpu.VMEM(PATCH, F32),
-            pltpu.VMEM((2, 5, *TILE), F32),
+            pltpu.VMEM((6, 5, *TILE), F32),
             pltpu.VMEM((6, *TILE), F32),
             pltpu.VMEM((3, 6, *TILE), F32),
-            pltpu.VMEM((6, 6, *TILE), F32),
-            DMA((8,)), DMA((8,)), DMA((4, 8)), DMA((4, 8)), DMA((32,)), DMA((32,)), DMA((3,)), DMA((3,)),
-            DMA((2, CHUNKS)), DMA((2, CHUNKS)), DMA((2, CHUNKS)), DMA((2, CHUNKS)),
-            DMA((CHUNKS,)), DMA((CHUNKS,)), DMA((CHUNKS,)), DMA((CHUNKS,)),
+            DMA((8,)), DMA((8,)), DMA((4, 8)), DMA, DMA((32,)), DMA((32,)), DMA((3,)), DMA((3,)),
+            DMA((2, PIECES)), DMA((2, PIECES)), DMA((2, PIECES)), DMA((2, PIECES)),
+            DMA((PIECES,)), DMA((PIECES,)), DMA((PIECES,)), DMA((PIECES,)),
         ],
         compiler_params=pltpu.CompilerParams(collective_id=0, has_side_effects=True, vmem_limit_bytes=LIMIT),
         name="step",
     )(partner, neighbours, work, link, fine_state, coarse_state)
 
 
-def write(fine_result, coarse_result):
+def finish(fine_result, coarse_result, amounts):
+    shape = jax.ShapeDtypeStruct(fine_result.shape, F32)
     return pl.pallas_call(
-        write_kernel,
-        out_shape=tuple(jax.ShapeDtypeStruct(v.shape, F32) for v in (fine_result, coarse_result)),
-        in_specs=[HBM, HBM],
+        finish_kernel,
+        out_shape=(shape, shape),
+        in_specs=[HBM, HBM, VMEM],
         out_specs=(HBM, HBM),
-        scratch_shapes=[DMA((2, 5))],
+        scratch_shapes=[
+            pltpu.VMEM((5, 32, 1024), F32), pltpu.VMEM(PATCH, F32), DMA((10,)), DMA((4,)), DMA((4, 8)),
+        ],
         compiler_params=pltpu.CompilerParams(vmem_limit_bytes=LIMIT),
-        name="write",
-    )(fine_result, coarse_result)
+        name="finish",
+    )(fine_result, coarse_result, amounts)
 
 
 def body(fine_state, coarse_state, partner, mig_slot, neighbours, work, coarse_link):
@@ -628,7 +695,7 @@
     results = step(
         partner.T, jnp.transpose(neighbours, (2, 1, 0)), work.T, coarse_link, fine_state, coarse_state
     )
-    return write(*results)
+    return finish(*results)
 
 
 def solution(mesh):

time: 101 us -> 54.2 us (0.54)
  Pallas kernels: 99 us -> 52.7 us
    pallas_call x1, Pallas kernels: 40.9 us -> 4.4 us  [finish(): pl.pallas_call(finish_kernel, out_shape=(shape, shape), in_specs=[HBM, HB...]
    pallas_call x1, Pallas kernels: 58.1 us -> 48.3 us  [step(): pl.pallas_call(step_kernel, out_shape=(jax.ShapeDtypeStruct(fine_state.sh...]
where the time goes in v5:
time: 54.2 us; the launch traced here: 53.9 us
  Pallas kernels  52.7 us (97%)
  between operations  1.29 us (2%)
    pallas_call x1, Pallas kernels, step(): pl.pallas_call(step_kernel, out_shape=(jax.ShapeDtypeStruct(fine_state.sh...  48.3 us
    pallas_call x1, Pallas kernels, finish(): pl.pallas_call(finish_kernel, out_shape=(shape, shape), in_specs=[HBM, HB...  4.4 us

profile of v5, /device:TPU:1, one launch (start us, length us, event | category | flops | bytes accessed | tf_op | source)
XLA Modules:
  0.0 53.9 jit_solution(10473415264079473798)
XLA Ops:
  1.3 48.3 %step.1 = (f32[1,1,5,32,1024]{4,3,2,1,0:T(8,128)}, f32[5,32,8,128]{3,2,1,0:T(8,128)}, f32[6,5,8,128]{3,2,1,0:T(8,128)}) custom-call(s32[1,32]{1,0:T(1,128)} %bitcast.4, s32[6,1,32]{2,1,0:T(1,128)} %bitcast.3, s32[1,32]{1,0:T(1,128)} %bitcast.5, s32[1,1]{1,0:T(1,128)S(6)} %copy.8.link, f32[1,1,5,32,1024]{4,3,2,1,0:T(8,128)} %fine.1, f32[1,1,5,32,1024]{4,3,2,1,0:T(8,128)} %coarse.1), custom_call_target="tpu_custom_call" | custom-call | tf_op jit(solution)/shard_map/step/pallas_call | solution.py:639
  49.5 4.4 %finish.1 = (f32[1,1,5,32,1024]{4,3,2,1,0:T(8,128)}, f32[1,1,5,32,1024]{4,3,2,1,0:T(8,128)}) custom-call(f32[1,1,5,32,1024]{4,3,2,1,0:T(8,128)} %get-tuple-element.5.fine, f32[5,32,8,128]{3,2,1,0:T(8,128)} %get-tuple-element.6.coarse, f32[6,5,8,128]{3,2,1,0:T(8,128)} %get-tuple-element.7.amounts), custom_call_target="tpu_custom_call" | custom-call | tf_op jit(solution)/shard_map/finish/pallas_call | solution.py:680

commit v6 on v5

--- a/solution.py
+++ b/solution.py
@@ -106,6 +106,10 @@
     lax.fori_loop(first, last, one, 0)
 
 
+def wait_for(ref, sem):
+    pltpu.make_async_copy(ref, ref, sem).wait()
+
+
 def load_plane(ref, x):
     return [ref[f, x] for f in range(5)]
 
@@ -174,7 +178,7 @@
     state, outer_y, outer_z, register, x_register, packed_z, carry, squeezed,
     coarse_state, flux_y, flux_z, flux_faces, note, notes,
     load_sem, coarse_sem, store_sem, coarse_store_sem, ghost_send, ghost_recv, note_send, note_recv,
-    near_send, near_recv, far_send, far_recv, up_send, up_recv, on_send, on_recv,
+    passed, reached, ended,
 ):
     slab = lax.axis_index("slab")
     lvl = lax.axis_index("lvl")
@@ -183,7 +187,7 @@
 
     def loads_of(source, target, sem):
         return [
-            pltpu.make_async_copy(source.at[0, 0, :, :, pl.ds(j * 128, 128)], target.at[:, :, j, :], sem.at[j])
+            pltpu.make_async_copy(source.at[0, 0, :, :, pl.ds(j * 128, 128)], target.at[:, :, j, :], sem)
             for j in range(8)
         ]
 
@@ -207,28 +211,28 @@
     def near(axis, piece):
         return pltpu.make_async_remote_copy(
             src_ref=span(own, piece), dst_ref=span(held.at[1 + 2 * axis], piece),
-            send_sem=near_send.at[axis, piece], recv_sem=near_recv.at[axis, piece],
+            send_sem=passed, recv_sem=reached.at[piece],
             device_id=(slab ^ (4 if axis else 1), lvl), device_id_type=MESH,
         )
 
     def far(axis, piece):
         return pltpu.make_async_remote_copy(
             src_ref=span(held.at[1 + 2 * axis], piece), dst_ref=span(held.at[2 + 2 * axis], piece),
-            send_sem=far_send.at[axis, piece], recv_sem=far_recv.at[axis, piece],
+            send_sem=passed, recv_sem=ended.at[piece],
             device_id=(slab ^ (12 if axis else 3), lvl), device_id_type=MESH,
         )
 
     def up(piece):
         return pltpu.make_async_remote_copy(
             src_ref=span(own, piece), dst_ref=span(relay, piece),
-            send_sem=up_send.at[piece], recv_sem=up_recv.at[piece],
+            send_sem=passed, recv_sem=reached.at[piece],
             device_id=(slab ^ (piece % 2 * 16), other_lvl), device_id_type=MESH,
         )
 
     def on(piece):
         return pltpu.make_async_remote_copy(
             src_ref=span(relay, piece), dst_ref=span(held.at[5], piece),
-            send_sem=on_send.at[piece], recv_sem=on_recv.at[piece],
+            send_sem=passed, recv_sem=ended.at[piece],
             device_id=(slab ^ ((piece + 1) % 2 * 16), other_lvl), device_id_type=MESH,
         )
 
@@ -237,11 +241,13 @@
         near(1, piece).start()
         up(piece).start()
 
+    def three(piece):
+        return held.at[pl.ds(0, 3), :, pl.ds(piece * PIECE, PIECE)]
+
     def forward(piece):
-        for axis in range(2):
-            near(axis, piece).wait_recv()
-            far(axis, piece).start()
-        up(piece).wait_recv()
+        wait_for(three(piece), reached.at[piece])
+        far(0, piece).start()
+        far(1, piece).start()
         on(piece).start()
 
     def relay_on(piece):
@@ -252,12 +258,9 @@
             send(piece + QUEUE)
 
     def arrive(piece):
-        far(0, piece).wait_recv()
-        far(1, piece).wait_recv()
-        on(piece).wait_recv()
-
-    for copy in fine_loads:
-        copy.wait()
+        wait_for(three(piece), ended.at[piece])
+
+    wait_for(own, load_sem)
     pl.semaphore_wait(barrier, 35)
     each(0, FIRST, send)
 
@@ -285,7 +288,7 @@
     def ghost(turn):
         return pltpu.make_async_remote_copy(
             src_ref=messages.at[turn], dst_ref=landed.at[turn],
-            send_sem=ghost_send.at[turn], recv_sem=ghost_recv.at[turn],
+            send_sem=ghost_send, recv_sem=ghost_recv,
             device_id=(slab ^ turn, lvl), device_id_type=MESH,
         )
 
@@ -297,8 +300,7 @@
     each(1, 32, send_ghost)
     each(FIRST, QUEUE, send)
 
-    for copy in coarse_loads:
-        copy.wait()
+    wait_for(coarse_state.at[:, pl.ds(1, 32)], coarse_sem)
     for f in range(5):
         coarse_state[f, 0] = coarse_state[f, 1]
         coarse_state[f, 33] = coarse_state[f, 32]
@@ -423,13 +425,13 @@
             pltpu.make_async_copy(
                 state.at[:, pl.ds(first + 1, 8), j, :],
                 fine_out.at[0, 0, :, pl.ds(first, 8), pl.ds(j * 128, 128)],
-                store_sem.at[piece, j],
+                store_sem,
             )
             for j in range(8)
         ]
 
     each(BESIDE, CHUNK // PIECE + AHEAD, relay_on)
-    each(1, 32, lambda turn: ghost(turn).wait_recv())
+    wait_for(landed.at[pl.ds(1, 31)], ghost_recv)
     for f in range(6):
         turn = jnp.maximum(linked[f], 0) ^ slab
         for i in range(5):
@@ -515,31 +517,21 @@
     place = level * 6 + (face ^ 1) + 1
     inside = (rows() // 4 == quarter_row) & (lanes() % 32 // 16 == quarter_col)
     note[5] = jnp.where(inside & valid, place.astype(F32), 0.0)
-    note_copies = []
     for turn in range(1, 4):
         copy = pltpu.make_async_remote_copy(
             src_ref=note, dst_ref=notes.at[turn - 1],
-            send_sem=note_send.at[turn - 1], recv_sem=note_recv.at[turn - 1],
+            send_sem=note_send, recv_sem=note_recv,
             device_id=(slab, lvl ^ turn), device_id_type=MESH,
         )
         copy.start()
-        note_copies.append(copy)
     for copy in stores_of(3):
         copy.start()
 
-    each(1, 32, lambda turn: ghost(turn).wait_send())
-
-    def sent(piece):
-        for axis in range(2):
-            near(axis, piece).wait_send()
-            far(axis, piece).wait_send()
-        up(piece).wait_send()
-        on(piece).wait_send()
-
-    each(0, PIECES, sent)
-
-    for copy in note_copies:
-        copy.wait_recv()
+    wait_for(messages.at[pl.ds(1, 31)], ghost_send)
+
+    wait_for(held, passed)
+
+    wait_for(notes, note_recv)
     for g in range(6):
         key = (lvl * 6 + g + 1).astype(F32)
         parts = [note if n == 3 else notes.at[n] for n in range(4)]
@@ -552,18 +544,14 @@
             for n in range(4):
                 total = total + jnp.where(hits[n], parts[n][f], 0.0)
             amounts[g, f] = (COARSE_STEP if g % 2 else -COARSE_STEP) * (cover * flux_faces[g, f] - total)
-    for copy in note_copies:
-        copy.wait_send()
+    wait_for(notes, note_send)
     coarse_store.wait()
-
-    def stored(piece):
-        for copy in stores_of(piece):
-            copy.wait()
-
-    each(0, 4, stored)
-
-
-def finish_kernel(fine, coarse, amounts, fine_out, coarse_out, fine_held, state, fine_sem, coarse_sem, out_sem):
+    wait_for(state.at[:, pl.ds(1, 32)], store_sem)
+
+
+def finish_kernel(
+    fine, coarse, amounts, fine_out, coarse_out, fine_held, state, fine_sem, fine_out_sem, coarse_sem, out_sem
+):
     def load(n):
         planes = pl.ds(n * 8, 8)
         return pltpu.make_async_copy(coarse.at[:, planes], state.at[:, planes], coarse_sem.at[n])
@@ -573,14 +561,14 @@
         return pltpu.make_async_copy(
             state.at[:, pl.ds(first, 8), j, :],
             coarse_out.at[0, 0, :, pl.ds(first, 8), pl.ds(j * 128, 128)],
-            out_sem.at[n, j],
+            out_sem,
         )
 
     def fine_load(f):
-        return pltpu.make_async_copy(fine.at[0, 0, f], fine_held.at[f], fine_sem.at[f])
+        return pltpu.make_async_copy(fine.at[0, 0, f], fine_held.at[f], fine_sem)
 
     def fine_store(f):
-        return pltpu.make_async_copy(fine_held.at[f], fine_out.at[0, 0, f], fine_sem.at[5 + f])
+        return pltpu.make_async_copy(fine_held.at[f], fine_out.at[0, 0, f], fine_out_sem)
 
     each(0, 4, lambda n: load(n).start())
     each(0, 5, lambda f: fine_load(f).start())
@@ -612,20 +600,12 @@
         for j in range(8):
             store(n, j).start()
 
-    def pass_on(f):
-        fine_load(f).wait()
-        fine_store(f).start()
-
     correct_eight(0)
-    each(0, 5, pass_on)
+    wait_for(fine_held, fine_sem)
+    each(0, 5, lambda f: fine_store(f).start())
     each(1, 4, correct_eight)
-    each(0, 5, lambda f: fine_store(f).wait())
-
-    def stored(n):
-        for j in range(8):
-            store(n, j).wait()
-
-    each(0, 4, stored)
+    wait_for(fine_held, fine_out_sem)
+    wait_for(state, out_sem)
 
 
 SMEM = pl.BlockSpec(memory_space=pltpu.SMEM)
@@ -666,9 +646,7 @@
             pltpu.VMEM((6, 5, *TILE), F32),
             pltpu.VMEM((6, *TILE), F32),
             pltpu.VMEM((3, 6, *TILE), F32),
-            DMA((8,)), DMA((8,)), DMA((4, 8)), DMA, DMA((32,)), DMA((32,)), DMA((3,)), DMA((3,)),
-            DMA((2, PIECES)), DMA((2, PIECES)), DMA((2, PIECES)), DMA((2, PIECES)),
-            DMA((PIECES,)), DMA((PIECES,)), DMA((PIECES,)), DMA((PIECES,)),
+            *(DMA,) * 9, DMA((PIECES,)), DMA((PIECES,)),
         ],
         compiler_params=pltpu.CompilerParams(collective_id=0, has_side_effects=True, vmem_limit_bytes=LIMIT),
         name="step",
@@ -683,7 +661,7 @@
         in_specs=[HBM, HBM, VMEM],
         out_specs=(HBM, HBM),
         scratch_shapes=[
-            pltpu.VMEM((5, 32, 1024), F32), pltpu.VMEM(PATCH, F32), DMA((10,)), DMA((4,)), DMA((4, 8)),
+            pltpu.VMEM((5, 32, 1024), F32), pltpu.VMEM(PATCH, F32), DMA, DMA, DMA((4,)), DMA,
         ],
         compiler_params=pltpu.CompilerParams(vmem_limit_bytes=LIMIT),
         name="finish",

time: 54.2 us -> 51.3 us (0.946)
  Pallas kernels: 52.7 us -> 49.8 us
    pallas_call x1, Pallas kernels: 48.3 us -> 45.8 us  [step(): pl.pallas_call(step_kernel, out_shape=(jax.ShapeDtypeStruct(fine_state.sh...]
where the time goes in v6:
time: 51.3 us; the launch traced here: 51.1 us
  Pallas kernels  49.8 us (97%)
  between operations  1.29 us (3%)
    pallas_call x1, Pallas kernels, step(): pl.pallas_call(step_kernel, out_shape=(jax.ShapeDtypeStruct(fine_state.sh...  45.8 us
    pallas_call x1, Pallas kernels, finish(): pl.pallas_call(finish_kernel, out_shape=(shape, shape), in_specs=[HBM, HB...  4.05 us

profile of v6, /device:TPU:1, one launch (start us, length us, event | category | flops | bytes accessed | tf_op | source)
XLA Modules:
  0.0 51.1 jit_solution(3590742699931567003)
XLA Ops:
  1.3 45.8 %step.1 = (f32[1,1,5,32,1024]{4,3,2,1,0:T(8,128)}, f32[5,32,8,128]{3,2,1,0:T(8,128)}, f32[6,5,8,128]{3,2,1,0:T(8,128)}) custom-call(s32[1,32]{1,0:T(1,128)} %bitcast.4, s32[6,1,32]{2,1,0:T(1,128)} %bitcast.3, s32[1,32]{1,0:T(1,128)} %bitcast.5, s32[1,1]{1,0:T(1,128)S(6)} %copy.8.link, f32[1,1,5,32,1024]{4,3,2,1,0:T(8,128)} %fine.1, f32[1,1,5,32,1024]{4,3,2,1,0:T(8,128)} %coarse.1), custom_call_target="tpu_custom_call" | custom-call | tf_op jit(solution)/shard_map/step/pallas_call | solution.py:619
  47.0 4.1 %finish.1 = (f32[1,1,5,32,1024]{4,3,2,1,0:T(8,128)}, f32[1,1,5,32,1024]{4,3,2,1,0:T(8,128)}) custom-call(f32[1,1,5,32,1024]{4,3,2,1,0:T(8,128)} %get-tuple-element.5.fine, f32[5,32,8,128]{3,2,1,0:T(8,128)} %get-tuple-element.6.coarse, f32[6,5,8,128]{3,2,1,0:T(8,128)} %get-tuple-element.7.amounts), custom_call_target="tpu_custom_call" | custom-call | tf_op jit(solution)/shard_map/finish/pallas_call | solution.py:658

commit v7 on v6

--- a/solution.py
+++ b/solution.py
@@ -550,7 +550,8 @@
 
 
 def finish_kernel(
-    fine, coarse, amounts, fine_out, coarse_out, fine_held, state, fine_sem, fine_out_sem, coarse_sem, out_sem
+    fine, coarse, given, fine_out, coarse_out, fine_held, state, amounts,
+    fine_sem, fine_out_sem, coarse_sem, given_sem, out_sem,
 ):
     def load(n):
         planes = pl.ds(n * 8, 8)
@@ -570,6 +571,8 @@
     def fine_store(f):
         return pltpu.make_async_copy(fine_held.at[f], fine_out.at[0, 0, f], fine_out_sem)
 
+    fetch = pltpu.make_async_copy(given, amounts, given_sem)
+    fetch.start()
     each(0, 4, lambda n: load(n).start())
     each(0, 5, lambda f: fine_load(f).start())
 
@@ -600,6 +603,7 @@
         for j in range(8):
             store(n, j).start()
 
+    fetch.wait()
     correct_eight(0)
     wait_for(fine_held, fine_sem)
     each(0, 5, lambda f: fine_store(f).start())
@@ -658,10 +662,11 @@
     return pl.pallas_call(
         finish_kernel,
         out_shape=(shape, shape),
-        in_specs=[HBM, HBM, VMEM],
+        in_specs=[HBM, HBM, HBM],
         out_specs=(HBM, HBM),
         scratch_shapes=[
-            pltpu.VMEM((5, 32, 1024), F32), pltpu.VMEM(PATCH, F32), DMA, DMA, DMA((4,)), DMA,
+            pltpu.VMEM((5, 32, 1024), F32), pltpu.VMEM(PATCH, F32), pltpu.VMEM((6, 5, *TILE), F32),
+            DMA, DMA, DMA((4,)), DMA, DMA,
         ],
         compiler_params=pltpu.CompilerParams(vmem_limit_bytes=LIMIT),
         name="finish",

time: 51.3 us -> 50.5 us (0.984)
  Pallas kernels: 49.8 us -> 49 us
    pallas_call x1, Pallas kernels: 4.05 us -> 3.2 us  [finish(): pl.pallas_call(finish_kernel, out_shape=(shape, shape), in_specs=[HBM, HB...]
where the time goes in v7:
time: 50.5 us; the launch traced here: 50.2 us
  Pallas kernels  49 us (97%)
  between operations  1.29 us (3%)
    pallas_call x1, Pallas kernels, step(): pl.pallas_call(step_kernel, out_shape=(jax.ShapeDtypeStruct(fine_state.sh...  45.8 us
    pallas_call x1, Pallas kernels, finish(): pl.pallas_call(finish_kernel, out_shape=(shape, shape), in_specs=[HBM, HB...  3.2 us

profile of v7, /device:TPU:1, one launch (start us, length us, event | category | flops | bytes accessed | tf_op | source)
XLA Modules:
  0.0 50.2 jit_solution(17337644799663404645)
XLA Ops:
  1.3 45.8 %step.1 = (f32[1,1,5,32,1024]{4,3,2,1,0:T(8,128)}, f32[5,32,8,128]{3,2,1,0:T(8,128)}, f32[6,5,8,128]{3,2,1,0:T(8,128)}) custom-call(s32[1,32]{1,0:T(1,128)} %bitcast.4, s32[6,1,32]{2,1,0:T(1,128)} %bitcast.3, s32[1,32]{1,0:T(1,128)} %bitcast.5, s32[1,1]{1,0:T(1,128)S(6)} %copy.8.link, f32[1,1,5,32,1024]{4,3,2,1,0:T(8,128)} %fine.1, f32[1,1,5,32,1024]{4,3,2,1,0:T(8,128)} %coarse.1), custom_call_target="tpu_custom_call" | custom-call | tf_op jit(solution)/shard_map/step/pallas_call | solution.py:623
  47.0 3.2 %finish.1 = (f32[1,1,5,32,1024]{4,3,2,1,0:T(8,128)}, f32[1,1,5,32,1024]{4,3,2,1,0:T(8,128)}) custom-call(f32[1,1,5,32,1024]{4,3,2,1,0:T(8,128)} %get-tuple-element.5.fine, f32[5,32,8,128]{3,2,1,0:T(8,128)} %get-tuple-element.6.coarse, f32[6,5,8,128]{3,2,1,0:T(8,128)} %get-tuple-element.7.given), custom_call_target="tpu_custom_call" | custom-call | tf_op jit(solution)/shard_map/finish/pallas_call | solution.py:662

commit v8 on v7

--- a/solution.py
+++ b/solution.py
@@ -512,12 +512,11 @@
         odd = squeezed[pl.ds(f * 8 + 1, 4, stride=2), :]
         small = jnp.where(low_lanes, even, pltpu.roll(odd, 64, 1))
         small = jnp.where(quarter_col == 0, small, pltpu.roll(small, 16, 1))
-        note[f, pl.ds(0, 4), :] = jnp.where(quarter_row == 0, small, 0.0)
-        note[f, pl.ds(4, 4), :] = jnp.where(quarter_row == 1, small, 0.0)
-    place = level * 6 + (face ^ 1) + 1
-    inside = (rows() // 4 == quarter_row) & (lanes() % 32 // 16 == quarter_col)
-    note[5] = jnp.where(inside & valid, place.astype(F32), 0.0)
-    for turn in range(1, 4):
+        note[f // 2, pl.ds(f % 2 * 4, 4), :] = small
+    place = (level * 6 + (face ^ 1)) * 2 + quarter_row + 1
+    columns = lax.broadcasted_iota(jnp.int32, (4, 128), 1) % 32 // 16
+    note[2, pl.ds(4, 4), :] = jnp.where((columns == quarter_col) & valid, place.astype(F32), 0.0)
+    for turn in (2, 3, 1):
         copy = pltpu.make_async_remote_copy(
             src_ref=note, dst_ref=notes.at[turn - 1],
             send_sem=note_send, recv_sem=note_recv,
@@ -532,18 +531,22 @@
     wait_for(held, passed)
 
     wait_for(notes, note_recv)
+    parts = [note if n == 3 else notes.at[n] for n in range(4)]
+    keys = [part[2, pl.ds(4, 4), :] for part in parts]
     for g in range(6):
-        key = (lvl * 6 + g + 1).astype(F32)
-        parts = [note if n == 3 else notes.at[n] for n in range(4)]
-        hits = [part[5] == key for part in parts]
-        cover = jnp.zeros(TILE, F32)
-        for n in range(4):
-            cover = cover + jnp.where(hits[n], 1.0, 0.0)
-        for f in range(5):
-            total = jnp.zeros(TILE, F32)
+        for half in range(2):
+            here = pl.ds(half * 4, 4)
+            key = ((lvl * 6 + g) * 2 + half + 1).astype(F32)
+            hits = [value == key for value in keys]
+            cover = jnp.zeros((4, 128), F32)
             for n in range(4):
-                total = total + jnp.where(hits[n], parts[n][f], 0.0)
-            amounts[g, f] = (COARSE_STEP if g % 2 else -COARSE_STEP) * (cover * flux_faces[g, f] - total)
+                cover = cover + jnp.where(hits[n], 1.0, 0.0)
+            for f in range(5):
+                total = jnp.zeros((4, 128), F32)
+                for n in range(4):
+                    total = total + jnp.where(hits[n], parts[n][f // 2, pl.ds(f % 2 * 4, 4), :], 0.0)
+                factor = COARSE_STEP if g % 2 else -COARSE_STEP
+                amounts[g, f, here, :] = factor * (cover * flux_faces[g, f, here, :] - total)
     wait_for(notes, note_send)
     coarse_store.wait()
     wait_for(state.at[:, pl.ds(1, 32)], store_sem)
@@ -648,8 +651,8 @@
             pltpu.VMEM(PATCH, F32),
             pltpu.VMEM(PATCH, F32),
             pltpu.VMEM((6, 5, *TILE), F32),
-            pltpu.VMEM((6, *TILE), F32),
-            pltpu.VMEM((3, 6, *TILE), F32),
+            pltpu.VMEM((3, *TILE), F32),
+            pltpu.VMEM((3, 3, *TILE), F32),
             *(DMA,) * 9, DMA((PIECES,)), DMA((PIECES,)),
         ],
         compiler_params=pltpu.CompilerParams(collective_id=0, has_side_effects=True, vmem_limit_bytes=LIMIT),

time: 50.5 us -> 50.4 us (level)
  no operation moved by 1% of the time
where the time goes in v8:
time: 50.4 us; the launch traced here: 50.2 us
  Pallas kernels  48.9 us (97%)
  between operations  1.29 us (3%)
    pallas_call x1, Pallas kernels, step(): pl.pallas_call(step_kernel, out_shape=(jax.ShapeDtypeStruct(fine_state.sh...  45.7 us
    pallas_call x1, Pallas kernels, finish(): pl.pallas_call(finish_kernel, out_shape=(shape, shape), in_specs=[HBM, HB...  3.2 us

profile of v8, /device:TPU:1, one launch (start us, length us, event | category | flops | bytes accessed | tf_op | source)
XLA Modules:
  0.0 50.2 jit_solution(12157259270011367255)
XLA Ops:
  1.3 45.7 %step.1 = (f32[1,1,5,32,1024]{4,3,2,1,0:T(8,128)}, f32[5,32,8,128]{3,2,1,0:T(8,128)}, f32[6,5,8,128]{3,2,1,0:T(8,128)}) custom-call(s32[1,32]{1,0:T(1,128)} %bitcast.4, s32[6,1,32]{2,1,0:T(1,128)} %bitcast.3, s32[1,32]{1,0:T(1,128)} %bitcast.5, s32[1,1]{1,0:T(1,128)S(6)} %copy.8.link, f32[1,1,5,32,1024]{4,3,2,1,0:T(8,128)} %fine.1, f32[1,1,5,32,1024]{4,3,2,1,0:T(8,128)} %coarse.1), custom_call_target="tpu_custom_call" | custom-call | tf_op jit(solution)/shard_map/step/pallas_call | solution.py:626
  47.0 3.2 %finish.1 = (f32[1,1,5,32,1024]{4,3,2,1,0:T(8,128)}, f32[1,1,5,32,1024]{4,3,2,1,0:T(8,128)}) custom-call(f32[1,1,5,32,1024]{4,3,2,1,0:T(8,128)} %get-tuple-element.5.fine, f32[5,32,8,128]{3,2,1,0:T(8,128)} %get-tuple-element.6.coarse, f32[6,5,8,128]{3,2,1,0:T(8,128)} %get-tuple-element.7.given), custom_call_target="tpu_custom_call" | custom-call | tf_op jit(solution)/shard_map/finish/pallas_call | solution.py:665
